TPU v7x, 32 devices: a whole 2x2x4 slice. The times are simulated.
32 devices in a mesh: groups: 2 (over x), tm: 16 (over z, y, core).
Axes of the slice: x: 2, y: 2, z: 4, core: 2. Of those that a mesh axis runs over, the one named last changes fastest.
Arguments:
- tokens: bfloat16 [2, 4096, 1152], P('groups', 'tm'), parts along dimension 0, may hold values from -6 to 6
- norm_gain: float32 [1152], replicated, may hold values from 0.5 to 8
- w_qkv: bfloat16 [1152, 1728], P('tm'), may hold values from -0.1875 to 0.1875
- w_out: bfloat16 [1152, 576], P('tm'), may hold values from -0.25 to 0.25
- block_mask: int32 [2, 2, 2], P('groups'), parts along dimension 0, may hold values from 0 to 1
- keep_tiles: int32 [2, 256], P('groups', 'tm'), parts along dimension 0, may hold values 0 or 1
- cotangent: bfloat16 [2, 4096, 1152], P('groups', 'tm'), parts along dimension 0, may hold values from -6 to 6
Outputs:
- mixed: bfloat16 [2, 4096, 1152], P('groups', 'tm'), parts along dimension 0
- grad_tokens: bfloat16 [2, 4096, 1152], P('groups', 'tm'), parts along dimension 0
- grad_qkv: float32 [2304, 1728], P(('groups', 'tm')), parts along dimension 0
- grad_out: float32 [2304, 576], P(('groups', 'tm')), parts along dimension 0
There are 2 independent parts, one for each index of `groups`. A program takes and returns all parts, laid end to end along the dimension named above; an argument that names none is the same for every part. Nothing has to cross between parts.
All inputs are finite; a program needn't handle non-finite values. No bound on the sum of `keep_tiles` on one device may be relied on, other than what follows from the above.
Results may differ from a plain program's by a relative error of at most 0.0055.
The roundings to bfloat16 on the way count: a program that leaves them out, or rounds other values in their place, can miss the bound.
Values may be sent and summed in bfloat16 or wider, within the bound.
A program may use at most 128 MiB of HBM per device.

v0:
```python
import jax
import jax.numpy as jnp
from jax import lax
from jax.sharding import PartitionSpec as P

HD = 72
SPLIT = 4
TB = 2
TILE = 16


EPS = 1e-06


def temporal(qkv_cols, dattn_cols, keep_cols, block_mask, frames):
    videos, per_owner, owners, _ = qkv_cols.shape
    band_count = owners // frames
    heads_n = dattn_cols.shape[-1] // HD
    scale = HD ** (-0.5)
    parts = qkv_cols.reshape(videos, per_owner, frames, band_count, 3, heads_n, HD)
    queries = parts[:, :, :, :, 0]
    key_part = parts[:, :, :, :, 1]
    val_part = parts[:, :, :, :, 2]
    d_out = dattn_cols.reshape(videos, per_owner, frames, band_count, heads_n, HD)
    frame_block = jnp.arange(frames) // TB
    blocks = jnp.repeat(jnp.repeat(block_mask, TB, 1), TB, 2) > 0
    same_block = frame_block[:, None] == frame_block[None, :]
    block_allow = blocks | same_block[None]
    kept = jnp.transpose(keep_cols.reshape(videos, per_owner, frames, band_count) > 0, (0, 1, 3, 2))
    diag_one = jnp.arange(frames)[:, None] == jnp.arange(frames)[None, :]
    allow = block_allow[:, None, None, None, :, :] & (kept[:, :, :, None, None, :] | diag_one)
    scores = (
        jnp.einsum("vrfshd,vrgshd->vrshfg", queries, key_part, preferred_element_type=jnp.float32)
        * scale
    )
    scores = jnp.where(allow, scores, -1e30)
    row_top = jnp.max(scores, -1, keepdims=True)
    expo = jnp.exp(scores - row_top)
    probs = expo / jnp.sum(expo, -1, keepdims=True)
    probs_b = probs.astype(jnp.bfloat16)
    attn = jnp.einsum(
        "vrshfg,vrgshd->vrfshd", probs_b, val_part, preferred_element_type=jnp.float32
    ).astype(jnp.bfloat16)
    dprob = jnp.einsum("vrfshd,vrgshd->vrshfg", d_out, val_part, preferred_element_type=jnp.float32)
    dscore = probs * (dprob - jnp.sum(probs * dprob, -1, keepdims=True))
    dscore_b = dscore.astype(jnp.bfloat16)
    grad_query = (
        jnp.einsum("vrshfg,vrgshd->vrfshd", dscore_b, key_part, preferred_element_type=jnp.float32)
        * scale
    ).astype(jnp.bfloat16)
    grad_key = (
        jnp.einsum("vrshfg,vrfshd->vrgshd", dscore_b, queries, preferred_element_type=jnp.float32)
        * scale
    ).astype(jnp.bfloat16)
    grad_value = jnp.einsum(
        "vrshfg,vrfshd->vrgshd", probs_b, d_out, preferred_element_type=jnp.float32
    ).astype(jnp.bfloat16)
    d_qkv = jnp.stack([grad_query, grad_key, grad_value], axis=4).reshape(
        videos, per_owner, owners, -1
    )
    return (attn.reshape(videos, per_owner, owners, -1), d_qkv)


def per_device(tokens, norm_gain, w_qkv, w_out, block_mask, keep_tiles, cotangent):
    owners = lax.axis_size("tm")
    videos, band_len, model_width = tokens.shape
    per_owner = band_len // owners
    frames = owners // SPLIT
    qkv_full, out_full = (
        lax.all_gather(w_qkv, "tm", axis=0, tiled=True),
        lax.all_gather(w_out, "tm", axis=0, tiled=True),
    )
    tok_float = tokens.astype(jnp.float32)
    inv_rms = lax.rsqrt(jnp.mean(tok_float * tok_float, -1, keepdims=True) + EPS)
    normed = tok_float * inv_rms
    hidden = (normed * norm_gain).astype(jnp.bfloat16)
    keep_tok = jnp.repeat(keep_tiles, TILE, axis=1).reshape(videos, per_owner, owners)
    qkv = jnp.dot(hidden, qkv_full, preferred_element_type=jnp.float32).astype(jnp.bfloat16)
    d_attn = jnp.dot(cotangent, out_full, preferred_element_type=jnp.float32).astype(jnp.bfloat16)
    qkv_cols, dattn_cols, keep_cols = (
        lax.all_to_all(
            qkv.reshape(videos, per_owner, owners, -1),
            "tm",
            split_axis=2,
            concat_axis=2,
            tiled=True,
        ),
        lax.all_to_all(
            d_attn.reshape(videos, per_owner, owners, -1),
            "tm",
            split_axis=2,
            concat_axis=2,
            tiled=True,
        ),
        lax.all_to_all(keep_tok, "tm", split_axis=2, concat_axis=2, tiled=True),
    )
    attn_cols, dqkv_cols = temporal(qkv_cols, dattn_cols, keep_cols, block_mask, frames)
    attn_rows, dqkv_rows = (
        lax.all_to_all(attn_cols, "tm", split_axis=2, concat_axis=2, tiled=True),
        lax.all_to_all(dqkv_cols, "tm", split_axis=2, concat_axis=2, tiled=True),
    )
    attn = attn_rows.reshape(videos, band_len, -1)
    d_qkv = dqkv_rows.reshape(videos, band_len, -1)
    part_qkv = jnp.einsum("vtd,vte->de", hidden, d_qkv, preferred_element_type=jnp.float32)
    part_out = jnp.einsum("vtd,vte->de", cotangent, attn, preferred_element_type=jnp.float32)
    d_hidden = lax.optimization_barrier(
        jnp.einsum("vte,de->vtd", d_qkv, qkv_full, preferred_element_type=jnp.float32).astype(
            jnp.bfloat16
        )
    )
    grad_qkv, grad_out = (
        lax.psum_scatter(part_qkv, "tm", scatter_dimension=0, tiled=True),
        lax.psum_scatter(part_out, "tm", scatter_dimension=0, tiled=True),
    )
    mixed = (
        tok_float + jnp.einsum("vte,de->vtd", attn, out_full, preferred_element_type=jnp.float32)
    ).astype(jnp.bfloat16)
    grad = d_hidden.astype(jnp.float32) * norm_gain
    grad_tokens = cotangent.astype(jnp.float32) + inv_rms * (
        grad - normed * jnp.mean(grad * normed, -1, keepdims=True)
    )
    return (mixed, grad_tokens.astype(jnp.bfloat16), grad_qkv, grad_out)


def solution(mesh):
    placed = (
        P("groups", "tm", None),
        P(),
        P("tm", None),
        P("tm", None),
        P("groups", None, None),
        P("groups", "tm"),
        P("groups", "tm", None),
    )
    return jax.shard_map(
        per_device,
        mesh=mesh,
        in_specs=placed,
        out_specs=(
            P("groups", "tm", None),
            P("groups", "tm", None),
            P(("groups", "tm"), None),
            P(("groups", "tm"), None),
        ),
        check_vma=False,
    )
```

profile of v0, /device:TPU:0, one launch (start us, length us, event | category | flops | bytes accessed | tf_op | source)
XLA Modules:
  0.0 400.1 jit_solution(6253478221850050072)
XLA Ops:
  9.9 7.4 %all-to-all-start.1 = ((s32[1,16,16]{1,0,2:T(1,128)}), s32[1,16,16]{1,0,2:T(1,128)S(1)}, u32[]{:S(2)}, u32[]{:S(2)}) async-start(s32[1,16,16]{1,0,2:T(1,128)} %broadcast_in_dim.16), calls=%async_computation.1 | async-start | bytes 16384 | tf_op jit(solution)/shard_map/all_to_all | solution.py:95
  18.6 33.7 %all-gather.5.cloned.1.call-done = bf16[1152,576]{1,0:T(8,128)(2,1)} async-done(((bf16[72,576]{1,0:T(8,128)(2,1)}), bf16[1152,576]{1,0:T(8,128)(2,1)}) %all-gather.5.cloned.1.call-update) | async-done | bytes 1327120 | tf_op jit(solution)/shard_map/all_gather | solution.py:71
  52.2 2.3 convolution_convert_fusion.4
  55.5 3.5 all-to-all-start.3
  59.1 48.6 %all-gather.3.cloned.1.call-done = bf16[1152,1728]{1,0:T(8,128)(2,1)} async-done(((bf16[72,1728]{1,0:T(8,128)(2,1)}), bf16[1152,1728]{1,0:T(8,128)(2,1)}) %all-gather.3.cloned.1.call-update) | async-done | bytes 3981328 | tf_op jit(solution)/shard_map/all_gather | solution.py:70
  107.7 4.0 convolution_convert_fusion.1
  113.6 3.9 all-to-all-start
  120.1 18.1 %all-to-all-done = bf16[1,16,16,1728]{3,1,0,2:T(8,128)(2,1)S(1)} async-done(((bf16[1,16,16,1728]{3,1,0,2:T(8,128)(2,1)}), bf16[1,16,16,1728]{3,1,0,2:T(8,128)(2,1)S(1)}, u32[]{:S(2)}, u32[]{:S(2)}) %all-to-all-start) | async-done | bytes 884768 | tf_op jit(solution)/shard_map/all_to_all | solution.py:81
  138.2 1.7 reshape.294
  141.4 3.1 fusion.35
  148.8 1.7 fusion.13
  151.7 6.1 %all-to-all-start.2 = ((bf16[1,16,16,576]{3,1,0,2:T(8,128)(2,1)}), bf16[1,16,16,576]{3,1,0,2:T(8,128)(2,1)S(1)}, u32[]{:S(2)}, u32[]{:S(2)}) async-start(bf16[1,16,16,576]{3,1,0,2:T(8,128)(2,1)} %reshape.289), calls=%async_computation.2 | async-start | bytes 655360 | tf_op jit(solution)/shard_map/all_to_all | solution.py:99
  157.8 1.8 fusion.15
  159.6 1.5 pad_maximum_fusion
  161.4 1.9 reshape.290
  163.3 5.6 %all-to-all-done.2 = bf16[1,16,16,576]{3,1,0,2:T(8,128)(2,1)S(1)} async-done(((bf16[1,16,16,576]{3,1,0,2:T(8,128)(2,1)}), bf16[1,16,16,576]{3,1,0,2:T(8,128)(2,1)S(1)}, u32[]{:S(2)}, u32[]{:S(2)}) %all-to-all-start.2) | async-done | bytes 294944 | tf_op jit(solution)/shard_map/all_to_all | solution.py:99
  168.9 3.6 all-to-all-start.4
  172.7 2.0 convolution_bitcast_fusion
  174.8 23.5 %all-to-all-done.4 = bf16[1,16,16,1728]{3,1,0,2:T(8,128)(2,1)S(1)} async-done(((bf16[1,16,16,1728]{3,1,0,2:T(8,128)(2,1)}), bf16[1,16,16,1728]{3,1,0,2:T(8,128)(2,1)S(1)}, u32[]{:S(2)}, u32[]{:S(2)}) %all-to-all-start.4) | async-done | bytes 884768 | tf_op jit(solution)/shard_map/all_to_all | solution.py:100
  199.5 4.6 %fusion.31 = f32[1152,1728]{1,0:T(8,128)} fusion(bf16[256,1728]{1,0:T(8,128)(2,1)S(1)} %bitcast.103, bf16[1,256,1152]{2,1,0:T(8,128)(2,1)S(1)} %copy-done, f32[1152]{0:T(1024)S(1)} %copy-done.10, f32[256]{0:T(256)S(1)} %add_rsqrt_fusion), kind=kOutput, calls=%fused_computation.51 | convolution fusion | flops 1020395520 | bytes 9442816 | tf_op jit(solution)/shard_map/vtd,vte->de/dot_general | solution.py:104
  206.0 1.5 fusion.2
  207.5 3.6 fusion.3
  212.7 73.5 %all-reduce.3.cloned.1.call-done = f32[1152,576]{0,1:T(8,128)} async-done(((f32[1152,576]{0,1:T(8,128)}), f32[1152,576]{0,1:T(8,128)}) %all-reduce.3.cloned.1.call-update) | async-done | bytes 2654224
  288.2 105.4 %reduce-scatter.3.cloned.1.call-done = f32[72,1728]{1,0:T(8,128)} async-done(((f32[1152,1728]{1,0:T(8,128)}), f32[72,1728]{1,0:T(8,128)}) %reduce-scatter.3.cloned.1.call-update) | async-done | bytes 497680 | tf_op jit(solution)/shard_map/reduce_scatter | solution.py:112
  (71 shorter events, 22.8 us)
Async XLA Ops:
  7.2 45.1 %all-gather.5.cloned.1.call-start = ((), (), s32[]{:S(2)}) async-start(), calls=%async_computation.7 | async-start | bytes 1566720 | tf_op jit(solution)/shard_map/all_gather | solution.py:71
  7.9 99.8 %all-gather.3.cloned.1.call-start = ((), (), s32[]{:S(2)}) async-start(), calls=%async_computation.6 | async-start | bytes 4386816 | tf_op jit(solution)/shard_map/all_gather | solution.py:70
  9.9 45.6 %all-to-all-start.1 = ((s32[1,16,16]{1,0,2:T(1,128)}), s32[1,16,16]{1,0,2:T(1,128)S(1)}, u32[]{:S(2)}, u32[]{:S(2)}) async-start(s32[1,16,16]{1,0,2:T(1,128)} %broadcast_in_dim.16), calls=%async_computation.1 | async-start | bytes 16384 | tf_op jit(solution)/shard_map/all_to_all | solution.py:95
  54.5 53.2 %copy-start = (bf16[1,256,1152]{2,1,0:T(8,128)(2,1)S(1)}, bf16[1,256,1152]{2,1,0:T(8,128)(2,1)}, u32[]{:S(2)}) copy-start(bf16[1,256,1152]{2,1,0:T(8,128)(2,1)} %param.7) | copy-start | bytes 1769476
  54.5 53.2 %copy-start.10 = (f32[1152]{0:T(1024)S(1)}, f32[1152]{0:T(1024)}, u32[]{:S(2)}) copy-start(f32[1152]{0:T(1024)} %param.8) | copy-start | bytes 13828
  55.5 58.1 %all-to-all-start.3 = ((bf16[1,16,16,576]{3,1,0,2:T(8,128)(2,1)}), bf16[1,16,16,576]{3,1,0,2:T(8,128)(2,1)S(1)}, u32[]{:S(2)}, u32[]{:S(2)}) async-start(bf16[1,16,16,576]{3,1,0,2:T(8,128)(2,1)} %copy.64), calls=%async_computation.3 | async-start | bytes 655360 | tf_op jit(solution)/shard_map/all_to_all | solution.py:88
  113.6 4.0 copy-start.11
  113.6 24.5 %all-to-all-start = ((bf16[1,16,16,1728]{3,1,0,2:T(8,128)(2,1)}), bf16[1,16,16,1728]{3,1,0,2:T(8,128)(2,1)S(1)}, u32[]{:S(2)}, u32[]{:S(2)}) async-start(bf16[1,16,16,1728]{3,1,0,2:T(8,128)(2,1)} %copy.51), calls=%async_computation | async-start | bytes 1835008 | tf_op jit(solution)/shard_map/all_to_all | solution.py:81
  141.4 3.1 copy-start.8
  144.4 2.6 copy-start.9
  144.4 1.1 copy-start.5
  147.0 1.0 copy-start.6
  151.7 17.2 %all-to-all-start.2 = ((bf16[1,16,16,576]{3,1,0,2:T(8,128)(2,1)}), bf16[1,16,16,576]{3,1,0,2:T(8,128)(2,1)S(1)}, u32[]{:S(2)}, u32[]{:S(2)}) async-start(bf16[1,16,16,576]{3,1,0,2:T(8,128)(2,1)} %reshape.289), calls=%async_computation.2 | async-start | bytes 655360 | tf_op jit(solution)/shard_map/all_to_all | solution.py:99
  157.8 1.8 copy-start.7
  163.3 9.4 %copy-start.2 = (bf16[1,256,1152]{2,1,0:T(8,128)(2,1)S(1)}, bf16[1,256,1152]{2,1,0:T(8,128)(2,1)}, u32[]{:S(2)}) copy-start(bf16[1,256,1152]{2,1,0:T(8,128)(2,1)} %param.13) | copy-start | bytes 1769476
  168.9 29.4 %all-to-all-start.4 = ((bf16[1,16,16,1728]{3,1,0,2:T(8,128)(2,1)}), bf16[1,16,16,1728]{3,1,0,2:T(8,128)(2,1)S(1)}, u32[]{:S(2)}, u32[]{:S(2)}) async-start(bf16[1,16,16,1728]{3,1,0,2:T(8,128)(2,1)} %reshape.290), calls=%async_computation.4 | async-start | bytes 1835008 | tf_op jit(solution)/shard_map/all_to_all | solution.py:100
  172.6 113.6 %all-reduce.3.cloned.1.call-start = ((), (), s32[]{:S(2)}) async-start(), calls=%async_computation.9 | async-start | bytes 5308416
  174.8 218.8 %reduce-scatter.3.cloned.1.call-start = ((), (), s32[]{:S(2)}) async-start(), calls=%async_computation.8 | async-start | bytes 8773632 | tf_op jit(solution)/shard_map/reduce_scatter | solution.py:112
  198.6 1.0 copy-start.3
  204.1 0.7 copy-start.12
  204.1 1.9 copy-start.1
  206.0 1.5 copy-start.4
Sparse Core Ops, SparseCore 0:
  10.1 42.0 all-gather.4
  54.5 53.1 all-gather.2
  177.0 109.1 all-reduce.2
  290.6 102.8 reduce-scatter.2
where the time goes:
time: 401 us; the launch traced here: 400 us
  waiting for transfers between devices  310 us (77%)
  matrix products  27.5 us (7%)
  starting transfers between devices  24.8 us (6%)
  local copies, waits for them, and re-layouts  17.5 us (4%)
  between operations  14.7 us (4%)
  other arithmetic  5.81 us (1%)
    reduce_scatter x1, waiting for transfers between devices, per_device(): lax.psum_scatter(part_qkv, 'tm', scatter_dimension=0, tiled=True)  105 us
    unnamed x5, waiting for transfers between devices  74.9 us
    all_gather x1, waiting for transfers between devices, per_device(): lax.all_gather(w_qkv, 'tm', axis=0, tiled=True)  48.6 us
    all_gather x1, waiting for transfers between devices, per_device(): lax.all_gather(w_out, 'tm', axis=0, tiled=True)  33.7 us
    all_to_all x1, waiting for transfers between devices, per_device(): lax.all_to_all(dqkv_cols, 'tm', split_axis=2, concat_axis=2, tiled=True)  23.5 us
    all_to_all x1, waiting for transfers between devices, per_device(): lax.all_to_all(qkv.reshape(videos, per_owner, owners, -1), 'tm', split_ax...  18.1 us
  transfers between devices with their start and end apart: 9, of which 7 were waited for; matrix products, arithmetic and copies ran while one was open for 9% of the time, Pallas kernels for 0%

commit v1 on v0

--- a/solution.py
+++ b/solution.py
@@ -1,6 +1,10 @@
+import functools
+
 import jax
 import jax.numpy as jnp
 from jax import lax
+from jax.experimental import pallas as pl
+from jax.experimental.pallas import tpu as pltpu
 from jax.sharding import PartitionSpec as P
 
 HD = 72
@@ -10,6 +14,8 @@
 
 
 EPS = 1e-06
+FRAMES_HERE = 4
+MESH = pl.DeviceIdType.MESH
 
 
 def temporal(qkv_cols, dattn_cols, keep_cols, block_mask, frames):
@@ -122,6 +128,394 @@
     return (mixed, grad_tokens.astype(jnp.bfloat16), grad_qkv, grad_out)
 
 
+def pid(x):
+    return {"tm": x}
+
+
+def place():
+    me = lax.axis_index("tm")
+    z, b = me // SPLIT, me % SPLIT
+    return me, z, b, b // 2, b % 2
+
+
+def greet(peers):
+    barrier = pltpu.get_barrier_semaphore()
+    for peer in peers:
+        pl.semaphore_signal(barrier, inc=1, device_id=peer, device_id_type=MESH)
+    pl.semaphore_wait(barrier, len(peers))
+
+
+def remote(src, dst, send_sem, recv_sem, peer):
+    return pltpu.make_async_remote_copy(
+        src_ref=src,
+        dst_ref=dst,
+        send_sem=send_sem,
+        recv_sem=recv_sem,
+        device_id=peer,
+        device_id_type=MESH,
+    )
+
+
+def gather_kernel(w_ref, out_ref, local_sem, send_z, send_y, send_x, send_c, recv):
+    x = lax.axis_index("groups")
+    me, z, b, y, c = place()
+    over_z = [pid((z + dz) % FRAMES_HERE * SPLIT + b) for dz in range(1, FRAMES_HERE)]
+    over_y = pid(z * SPLIT + (1 - y) * 2 + c)
+    over_c = pid(z * SPLIT + y * 2 + (1 - c))
+    over_x = {"groups": 1 - x}
+    greet(over_z + [over_y, over_c, over_x])
+    mine = (x, 2)
+    started = []
+
+    def send(src, t, k, sem, peer):
+        copy = remote(src, out_ref.at[t, k], sem, recv.at[t, k], peer)
+        copy.start()
+        started.append(copy)
+
+    def arrived(t, k, peer):
+        remote(out_ref.at[t, k], out_ref.at[t, k], send_z.at[0, 0], recv.at[t, k], peer).wait_recv()
+
+    local = [
+        pltpu.make_async_copy(w_ref.at[t], out_ref.at[t, me], local_sem.at[i])
+        for i, t in enumerate(mine)
+    ]
+    for copy in local:
+        copy.start()
+    for dz in range(1, FRAMES_HERE):
+        for i, t in enumerate(mine):
+            send(w_ref.at[t], t, me, send_z.at[i, dz], over_z[dz - 1])
+    shards = [(z + FRAMES_HERE - dz) % FRAMES_HERE * SPLIT for dz in range(FRAMES_HERE)]
+    order = [0, 1, 3, 2]
+    for dz in order:
+        k = shards[dz] + b
+        for i, t in enumerate(mine):
+            if dz:
+                arrived(t, k, over_y)
+            src = out_ref.at[t, k] if dz else w_ref.at[t]
+            send(src, t, k, send_y.at[i, dz], over_y)
+            if i == 0:
+                send(src, t, k, send_x.at[0, dz], over_x)
+            send(src, t, k, send_c.at[i, 0, dz], over_c)
+    for dz in order:
+        k = shards[dz] + (1 - y) * 2 + c
+        for i, t in enumerate(mine):
+            arrived(t, k, over_y)
+            if i == 0:
+                send(out_ref.at[t, k], t, k, send_x.at[1, dz], over_x)
+            send(out_ref.at[t, k], t, k, send_c.at[i, 1, dz], over_c)
+    for j in range(2):
+        for dz in order:
+            k = shards[dz] + (y if j == 0 else 1 - y) * 2 + c
+            arrived(1 - x, k, over_x)
+            send(out_ref.at[1 - x, k], 1 - x, k, send_c.at[2, j, dz], over_c)
+    for t in range(3):
+        for yy in range(2):
+            for zz in range(FRAMES_HERE):
+                arrived(t, zz * SPLIT + yy * 2 + (1 - c), over_c)
+    for copy in local:
+        copy.wait()
+    for copy in started:
+        copy.wait_send()
+
+
+def gather_weights(blocks):
+    owners = FRAMES_HERE * SPLIT
+    dma = pltpu.SemaphoreType.DMA
+    return pl.pallas_call(
+        gather_kernel,
+        out_shape=jax.ShapeDtypeStruct((3, owners) + blocks.shape[1:], blocks.dtype),
+        in_specs=[pl.BlockSpec(memory_space=pl.ANY)],
+        out_specs=pl.BlockSpec(memory_space=pl.ANY),
+        scratch_shapes=[
+            dma((2,)),
+            dma((2, FRAMES_HERE)),
+            dma((2, FRAMES_HERE)),
+            dma((2, FRAMES_HERE)),
+            dma((3, 2, FRAMES_HERE)),
+            dma((3, owners)),
+        ],
+        compiler_params=pltpu.CompilerParams(collective_id=0, has_side_effects=True),
+    )(blocks)
+
+
+def forward_kernel(
+    pay, keep, cols, pay_out, keep_out, cols_out, local_sem, send_z, recv_z, send_b, recv_b
+):
+    me, z, b, y, c = place()
+    over_z = [pid((z + dz) % FRAMES_HERE * SPLIT + b) for dz in range(1, FRAMES_HERE)]
+    over_b = [pid(z * SPLIT + (b + db) % SPLIT) for db in range(1, SPLIT)]
+    greet(over_z + over_b)
+    local = [
+        pltpu.make_async_copy(pay.at[z], pay_out.at[z], local_sem.at[0]),
+        pltpu.make_async_copy(keep.at[z], keep_out.at[z], local_sem.at[1]),
+        pltpu.make_async_copy(cols.at[b], cols_out.at[b], local_sem.at[2]),
+    ]
+    copies = []
+    for dz in (2, 1, 3):
+        to = (z + dz) % FRAMES_HERE
+        peer = over_z[dz - 1]
+        copies.append(remote(keep.at[to], keep_out.at[z], send_z.at[1, dz], recv_z.at[1, dz], peer))
+        copies.append(remote(pay.at[to], pay_out.at[z], send_z.at[0, dz], recv_z.at[0, dz], peer))
+    for db in (2, 1, 3):
+        to = (b + db) % SPLIT
+        copies.append(
+            remote(cols.at[to], cols_out.at[b], send_b.at[db], recv_b.at[db], over_b[db - 1])
+        )
+    for copy in copies + local:
+        copy.start()
+    for dz in (1, 2, 3):
+        came = (z + FRAMES_HERE - dz) % FRAMES_HERE
+        peer = over_z[dz - 1]
+        remote(keep.at[z], keep_out.at[came], send_z.at[1, dz], recv_z.at[1, dz], peer).wait_recv()
+        remote(pay.at[z], pay_out.at[came], send_z.at[0, dz], recv_z.at[0, dz], peer).wait_recv()
+    for db in (1, 2, 3):
+        came = (b + SPLIT - db) % SPLIT
+        remote(cols.at[b], cols_out.at[came], send_b.at[db], recv_b.at[db], over_b[db - 1]).wait_recv()
+    for copy in local:
+        copy.wait()
+    for copy in copies:
+        copy.wait_send()
+
+
+def send_forward(pay, keep, cols):
+    dma = pltpu.SemaphoreType.DMA
+    return pl.pallas_call(
+        forward_kernel,
+        out_shape=[jax.ShapeDtypeStruct(a.shape, a.dtype) for a in (pay, keep, cols)],
+        in_specs=[pl.BlockSpec(memory_space=pl.ANY)] * 3,
+        out_specs=[pl.BlockSpec(memory_space=pl.ANY)] * 3,
+        scratch_shapes=[dma((3,)), dma((2, 4)), dma((2, 4)), dma((4,)), dma((4,))],
+        compiler_params=pltpu.CompilerParams(collective_id=1, has_side_effects=True),
+    )(pay, keep, cols)
+
+
+def back_kernel(res, out, local_sem, send_z, send_y, send_c, recv):
+    me, z, b, y, c = place()
+    over_z = [pid((z + dz) % FRAMES_HERE * SPLIT + b) for dz in range(1, FRAMES_HERE)]
+    over_y = pid(z * SPLIT + (1 - y) * 2 + c)
+    over_c = pid(z * SPLIT + y * 2 + (1 - c))
+    greet(over_z + [over_y, over_c])
+    started = []
+
+    def send(src, i, j, sem, peer):
+        copy = remote(src, out.at[i, j], sem, recv.at[i, j], peer)
+        copy.start()
+        started.append(copy)
+
+    def arrived(i, j, peer):
+        remote(out.at[i, j], out.at[i, j], send_z.at[0], recv.at[i, j], peer).wait_recv()
+
+    local = pltpu.make_async_copy(res.at[z], out.at[b, z], local_sem)
+    local.start()
+    for dz in (2, 1, 3):
+        send(res.at[(z + dz) % FRAMES_HERE], b, z, send_z.at[dz], over_z[dz - 1])
+    order = [0, 1, 3, 2]
+    for dz in order:
+        j = (z + FRAMES_HERE - dz) % FRAMES_HERE
+        if dz:
+            arrived(b, j, over_y)
+        src = out.at[b, j] if dz else res.at[z]
+        send(src, b, j, send_y.at[dz], over_y)
+        send(src, b, j, send_c.at[0, dz], over_c)
+    for dz in order:
+        i, j = (1 - y) * 2 + c, (z + FRAMES_HERE - dz) % FRAMES_HERE
+        arrived(i, j, over_y)
+        send(out.at[i, j], i, j, send_c.at[1, dz], over_c)
+    for yy in range(2):
+        for j in range(FRAMES_HERE):
+            arrived(yy * 2 + (1 - c), j, over_c)
+    local.wait()
+    for copy in started:
+        copy.wait_send()
+
+
+def send_back(res):
+    dma = pltpu.SemaphoreType.DMA
+    return pl.pallas_call(
+        back_kernel,
+        out_shape=jax.ShapeDtypeStruct((SPLIT,) + res.shape, res.dtype),
+        in_specs=[pl.BlockSpec(memory_space=pl.ANY)],
+        out_specs=pl.BlockSpec(memory_space=pl.ANY),
+        scratch_shapes=[dma, dma((4,)), dma((4,)), dma((2, 4)), dma((4, 4))],
+        compiler_params=pltpu.CompilerParams(collective_id=2, has_side_effects=True),
+    )(res)
+
+
+def sums_kernel(part, out, local_sem, send_z, recv_z):
+    me, z, b, y, c = place()
+    over_z = [pid((z + dz) % FRAMES_HERE * SPLIT + b) for dz in range(1, FRAMES_HERE)]
+    greet(over_z)
+    local = pltpu.make_async_copy(part.at[z], out.at[z], local_sem)
+    copies = [
+        remote(
+            part.at[(z + dz) % FRAMES_HERE],
+            out.at[z],
+            send_z.at[dz],
+            recv_z.at[dz],
+            over_z[dz - 1],
+        )
+        for dz in (2, 1, 3)
+    ]
+    for copy in copies + [local]:
+        copy.start()
+    for dz in (1, 2, 3):
+        came = (z + FRAMES_HERE - dz) % FRAMES_HERE
+        remote(part.at[z], out.at[came], send_z.at[dz], recv_z.at[dz], over_z[dz - 1]).wait_recv()
+    local.wait()
+    for copy in copies:
+        copy.wait_send()
+
+
+def send_sums(part):
+    dma = pltpu.SemaphoreType.DMA
+    return pl.pallas_call(
+        sums_kernel,
+        out_shape=jax.ShapeDtypeStruct(part.shape, part.dtype),
+        in_specs=[pl.BlockSpec(memory_space=pl.ANY)],
+        out_specs=pl.BlockSpec(memory_space=pl.ANY),
+        scratch_shapes=[dma, dma((4,)), dma((4,))],
+        compiler_params=pltpu.CompilerParams(collective_id=3, has_side_effects=True),
+    )(part)
+
+
+def attention_kernel(pay, allow, out, dk_sum, dv_sum):
+    f32, bf16 = jnp.float32, jnp.bfloat16
+    width = pay.shape[-1] // 4
+    rows = pay.shape[1]
+    scale = HD ** (-0.5)
+    frames = pay.shape[0]
+    row = lax.broadcasted_iota(jnp.int32, (width, 128), 0)
+    lane = lax.broadcasted_iota(jnp.int32, (width, 128), 1)
+    gather = ((row >= lane * HD) & (row < lane * HD + HD)).astype(f32).astype(bf16)
+    row_t = lax.broadcasted_iota(jnp.int32, (128, width), 1)
+    lane_t = lax.broadcasted_iota(jnp.int32, (128, width), 0)
+    spread = ((row_t >= lane_t * HD) & (row_t < lane_t * HD + HD)).astype(f32).astype(bf16)
+
+    def part(i, f):
+        return pay[f, :, i * width : (i + 1) * width].astype(f32)
+
+    def head_sums(prod):
+        high = prod.astype(bf16)
+        low = (prod - high.astype(f32)).astype(bf16)
+        return jnp.dot(high, gather, preferred_element_type=f32) + jnp.dot(
+            low, gather, preferred_element_type=f32
+        )
+
+    for f in range(frames):
+        query, d_out = part(0, f), part(3, f)
+        scores, dprob = [], []
+        for g in range(frames):
+            raw = head_sums(query * part(1, g)) * scale
+            scores.append(jnp.where(allow[f * frames + g] > 0, raw, -1e30))
+            dprob.append(head_sums(d_out * part(2, g)))
+        top = functools.reduce(jnp.maximum, scores)
+        expo = [jnp.exp(s - top) for s in scores]
+        total = functools.reduce(jnp.add, expo)
+        probs = [e / total for e in expo]
+        inner = functools.reduce(jnp.add, [p * d for p, d in zip(probs, dprob)])
+        attn = jnp.zeros((rows, width), f32)
+        d_query = jnp.zeros((rows, width), f32)
+        for g in range(frames):
+            pb = jnp.dot(probs[g].astype(bf16), spread, preferred_element_type=f32)
+            dscore = (probs[g] * (dprob[g] - inner)).astype(bf16)
+            ds = jnp.dot(dscore, spread, preferred_element_type=f32)
+            attn += pb * part(2, g)
+            d_query += ds * part(1, g)
+            if f == 0:
+                dk_sum[g] = ds * query
+                dv_sum[g] = pb * d_out
+            else:
+                dk_sum[g] += ds * query
+                dv_sum[g] += pb * d_out
+        out[f, :, 0:width] = attn.astype(bf16)
+        out[f, :, width : 2 * width] = (d_query * scale).astype(bf16)
+    for g in range(frames):
+        out[g, :, 2 * width : 3 * width] = (dk_sum[g] * scale).astype(bf16)
+        out[g, :, 3 * width : 4 * width] = dv_sum[g].astype(bf16)
+
+
+def attention(pay, allow):
+    frames, rows, wide = pay.shape
+    return pl.pallas_call(
+        attention_kernel,
+        out_shape=jax.ShapeDtypeStruct(pay.shape, pay.dtype),
+        in_specs=[pl.BlockSpec(memory_space=pltpu.VMEM)] * 2,
+        out_specs=pl.BlockSpec(memory_space=pltpu.VMEM),
+        scratch_shapes=[pltpu.VMEM((frames, rows, wide // 4), jnp.float32)] * 2,
+        compiler_params=pltpu.CompilerParams(vmem_limit_bytes=32 * 1024 * 1024),
+    )(pay, allow)
+
+
+def four_frames(tokens, norm_gain, w_qkv, w_out, block_mask, keep_tiles, cotangent):
+    f32, bf16 = jnp.float32, jnp.bfloat16
+    frames = FRAMES_HERE
+    tokens, cotangent = tokens[0], cotangent[0]
+    band, model = tokens.shape
+    shard, wide_qkv = w_qkv.shape
+    wide = wide_qkv + w_out.shape[1]
+    rows = band // frames
+    blocks = jnp.concatenate([w_qkv, w_out], 1).reshape(shard, 3, wide // 3).transpose(1, 0, 2)
+    weights = gather_weights(blocks)
+    weights = weights.transpose(1, 2, 0, 3).reshape(model, wide)
+    qkv_full, out_full = weights[:, :wide_qkv], weights[:, wide_qkv:]
+
+    tok_float = tokens.astype(f32)
+    inv_rms = lax.rsqrt(jnp.mean(tok_float * tok_float, -1, keepdims=True) + EPS)
+    normed = tok_float * inv_rms
+    hidden = (normed * norm_gain).astype(bf16)
+    qkv = jnp.dot(hidden, qkv_full, preferred_element_type=f32).astype(bf16)
+    d_attn = jnp.dot(cotangent, out_full, preferred_element_type=f32).astype(bf16)
+    pay = jnp.concatenate([qkv, d_attn], 1).reshape(frames, rows, wide)
+    keep = jnp.repeat(keep_tiles[0].astype(f32), TILE).reshape(frames, 1, rows)
+    keep = jnp.pad(jnp.broadcast_to(keep, (frames, 8, rows)), ((0, 0), (0, 0), (0, 128 - rows)))
+
+    def owners_columns(a):
+        return a.reshape(band, frames, SPLIT, shard).transpose(2, 0, 1, 3).reshape(SPLIT, band, -1)
+
+    cols = jnp.concatenate([owners_columns(hidden), owners_columns(cotangent)], 2)
+    pay_at, keep_at, cols_at = send_forward(pay, keep, cols)
+
+    frame_block = jnp.arange(frames) // TB
+    same_block = frame_block[:, None] == frame_block[None, :]
+    seen = (jnp.repeat(jnp.repeat(block_mask[0], TB, 0), TB, 1) > 0) | same_block
+    diag_one = jnp.arange(frames)[:, None] == jnp.arange(frames)[None, :]
+    kept = keep_at[:, 0, :rows] > 0
+    allow = seen[:, :, None] & (kept[None] | diag_one[:, :, None])
+    allow = jnp.broadcast_to(
+        allow.reshape(frames * frames, rows, 1).astype(f32), (frames * frames, rows, 128)
+    )
+    res = send_back(attention(pay_at, allow))
+
+    res_all = res.reshape(SPLIT * band, wide)
+    width = wide // 4
+    mine = lax.dynamic_index_in_dim(res, lax.axis_index("tm") % SPLIT, 0, keepdims=False)
+    mine = mine.reshape(band, wide)
+    attn, d_qkv = mine[:, :width], mine[:, width:]
+    cols_all = cols_at.reshape(SPLIT * band, -1)
+    half = cols_all.shape[1] // 2
+    part_qkv = jnp.einsum(
+        "td,te->de", cols_all[:, :half], res_all[:, width:], preferred_element_type=f32
+    )
+    part_out = jnp.einsum(
+        "td,te->de", cols_all[:, half:], res_all[:, :width], preferred_element_type=f32
+    )
+    parts = jnp.concatenate([part_qkv, part_out], 1).reshape(frames, shard, wide)
+    sums = jnp.sum(send_sums(parts), 0)
+    grad_qkv, grad_out = sums[:, :wide_qkv], sums[:, wide_qkv:]
+
+    d_hidden = lax.optimization_barrier(
+        jnp.einsum("te,de->td", d_qkv, qkv_full, preferred_element_type=f32).astype(bf16)
+    )
+    mixed = (
+        tok_float + jnp.einsum("te,de->td", attn, out_full, preferred_element_type=f32)
+    ).astype(bf16)
+    grad = d_hidden.astype(f32) * norm_gain
+    grad_tokens = cotangent.astype(f32) + inv_rms * (
+        grad - normed * jnp.mean(grad * normed, -1, keepdims=True)
+    )
+    return (mixed[None], grad_tokens.astype(bf16)[None], grad_qkv, grad_out)
+
+
 def solution(mesh):
     placed = (
         P("groups", "tm", None),
@@ -132,8 +526,9 @@
         P("groups", "tm"),
         P("groups", "tm", None),
     )
+    small = mesh.shape["tm"] == FRAMES_HERE * SPLIT and mesh.shape["groups"] == 2
     return jax.shard_map(
-        per_device,
+        four_frames if small else per_device,
         mesh=mesh,
         in_specs=placed,
         out_specs=(

time: 401 us -> 235 us (0.59)
  the two profiles are of different devices: /device:TPU:0 before, /device:TPU:16 now
where the time goes in v1:
time: 235 us; the launch traced here: 234 us
  Pallas kernels  185 us (79%)
  local copies, waits for them, and re-layouts  27.1 us (12%)
  matrix products  12.5 us (5%)
  other arithmetic  9.35 us (4%)
    pallas_call x1, Pallas kernels, send_sums(): pl.pallas_call(sums_kernel, out_shape=jax.ShapeDtypeStruct(part.shape, pa...  60.3 us
    pallas_call x1, Pallas kernels, send_back(): pl.pallas_call(back_kernel, out_shape=jax.ShapeDtypeStruct((SPLIT,) + res...  50.4 us
    pallas_call x1, Pallas kernels, gather_weights(): pl.pallas_call(gather_kernel, out_shape=jax.ShapeDtypeStruct((3, owners)...  35 us
    pallas_call x1, Pallas kernels, send_forward(): pl.pallas_call(forward_kernel, out_shape=[jax.ShapeDtypeStruct(a.shape, a...  33.8 us
    transpose x1, local copies, waits for them, and re-layouts, four_frames(): weights = weights.transpose(1, 2, 0, 3).reshape(model, wide)  9.97 us
    unnamed x25, local copies, waits for them, and re-layouts  7.32 us
    pallas_call x1, Pallas kernels, attention(): pl.pallas_call(attention_kernel, out_shape=jax.ShapeDtypeStruct(pay.shape...  5.01 us

profile of v1, /device:TPU:16, one launch (start us, length us, event | category | flops | bytes accessed | tf_op | source)
XLA Modules:
  0.0 234.4 jit_solution(11796014375968738262)
XLA Ops:
  0.6 1.1 pad_maximum_fusion.3
  2.5 35.0 %shard_map.102 = bf16[3,16,72,768]{3,2,1,0:T(8,128)(2,1)} custom-call(bf16[3,72,768]{2,1,0:T(8,128)(2,1)} %bitcast.73), custom_call_target="tpu_custom_call" | custom-call | tf_op jit(solution)/shard_map/pallas_call | solution.py:224
  37.5 10.0 %copy.15 = bf16[16,72,3,768]{3,2,1,0:T(4,128)(2,1)} copy(bf16[16,72,3,768]{3,1,0,2:T(8,128)(2,1)} %bitcast.58) | data formatting | bytes 10616832 | tf_op jit(solution)/shard_map/transpose | solution.py:459
  47.5 4.4 %copy.25 = bf16[144,8,3,768]{3,1,2,0:T(8,128)(2,1)S(1)} copy(bf16[144,8,3,768]{3,2,1,0:T(4,128)(2,1)} %bitcast.57) | data formatting | bytes 10616832
  51.9 1.2 fusion.23
  53.6 1.9 fusion.7
  55.7 1.5 copy.16
  59.3 0.9 copy.18
  60.2 1.4 copy.21
  61.6 1.6 pad_maximum_fusion.1.cols
  63.1 33.8 %shard_map.103 = (bf16[4,64,2304]{2,1,0:T(8,128)(2,1)}, f32[4,8,128]{2,1,0:T(8,128)}, bf16[4,256,576]{2,1,0:T(8,128)(2,1)}) custom-call(bf16[4,64,2304]{2,1,0:T(8,128)(2,1)} %bitcast.68, f32[4,8,128]{2,1,0:T(8,128)} %pad.4.keep, bf16[4,256,576]{2,1,0:T(8,128)(2,1)} %pad_maximum_fusion.1.cols), custom_call_target="tpu_custom_call" | custom-call | tf_op jit(solution)/shard_map/pallas_call | solution.py:282
  98.6 1.3 copy-done.1
  99.8 5.0 %shard_map.104.res = bf16[4,64,2304]{2,1,0:T(8,128)(2,1)S(1)} custom-call(bf16[4,64,2304]{2,1,0:T(8,128)(2,1)S(1)} %copy-done.1, f32[16,64,128]{2,1,0:T(8,128)S(1)} %broadcast_in_dim.21.allow), custom_call_target="tpu_custom_call" | custom-call | tf_op jit(solution)/shard_map/pallas_call | solution.py:439
  104.9 1.0 copy-done
  105.9 50.4 %shard_map.105 = bf16[4,4,64,2304]{3,2,1,0:T(8,128)(2,1)} custom-call(bf16[4,64,2304]{2,1,0:T(8,128)(2,1)} %copy-done), custom_call_target="tpu_custom_call" | custom-call | tf_op jit(solution)/shard_map/pallas_call | solution.py:334
  156.3 1.4 constant_dynamic-slice_fusion
  157.6 3.2 %fusion.13 = bf16[1,256,1152]{2,1,0:T(8,128)(2,1)} fusion(bf16[1152,2304]{1,0:T(8,128)(2,1)} %bitcast.66, bf16[1,256,1152]{2,1,0:T(8,128)(2,1)S(1)} %copy-done.2, bf16[256,2304]{1,0:T(8,128)(2,1)S(1)} %bitcast.75), kind=kOutput, calls=%fused_computation.11 | convolution fusion | flops 340623360 | bytes 2981888 | tf_op jit(solution)/shard_map/te,de->td/dot_general | solution.py:510
  160.8 3.6 %fusion.10 = bf16[256,1152]{1,0:T(8,128)(2,1)S(1)} fusion(bf16[1152,2304]{1,0:T(8,128)(2,1)} %bitcast.67, bf16[256,2304]{1,0:T(8,128)(2,1)S(1)} %bitcast.76), kind=kOutput, calls=%fused_computation.10 | convolution fusion | flops 1019510784 | bytes 5636096 | tf_op jit(solution)/shard_map/te,de->td/dot_general | solution.py:507
  164.8 1.2 fusion.30
  166.1 0.9 fusion.14
  167.0 1.7 fusion
  168.7 1.8 pad_maximum_fusion
  170.5 60.3 %shard_map.106 = f32[4,72,2304]{2,1,0:T(8,128)} custom-call(f32[4,72,2304]{2,1,0:T(8,128)} %bitcast.59), custom_call_target="tpu_custom_call" | custom-call | tf_op jit(solution)/shard_map/pallas_call | solution.py:371
  230.8 2.0 reduce_sum.29
  (59 shorter events, 7.0 us)
Async XLA Ops:
  47.5 4.4 %copy-start.4 = (bf16[1,256,1152]{2,1,0:T(8,128)(2,1)S(1)}, bf16[1,256,1152]{2,1,0:T(8,128)(2,1)}, u32[]{:S(2)}) copy-start(bf16[1,256,1152]{2,1,0:T(8,128)(2,1)} %param.13) | copy-start | bytes 1769476
  51.9 3.7 %copy-start.3 = (bf16[144,8,3,768]{3,1,2,0:T(8,128)(2,1)}, bf16[144,8,3,768]{3,1,2,0:T(8,128)(2,1)S(1)}, u32[]{:S(2)}) copy-start(bf16[144,8,3,768]{3,1,2,0:T(8,128)(2,1)S(1)} %copy.25) | copy-start | bytes 15925252
  51.9 1.5 copy-start.2
  51.9 1.7 copy-start.5
  55.6 1.5 copy-start.8
  63.1 34.7 %copy-start.7 = (s32[1,2,2]{2,1,0:T(2,128)S(1)}, s32[1,2,2]{2,1,0:T(2,128)}, u32[]{:S(2)}) copy-start(s32[1,2,2]{2,1,0:T(2,128)} %param.11) | copy-start | bytes 52
  98.6 1.3 copy-start.1
  104.9 1.0 copy-start
  157.6 8.4 %slice-start = ((s8[4718592]{0:T(1024)(128)(4,1)}), s8[4194304]{0:T(1024)(128)(4,1)S(1)}, s32[]{:S(2)}) async-start(s8[4718592]{0:T(1024)(128)(4,1)} %bitcast.60), calls=%async_computation | async-start | bytes 8388608
  160.8 5.2 %slice-start.1 = ((s8[4718592]{0:T(1024)(128)(4,1)}), s8[524288]{0:T(1024)(128)(4,1)S(1)}, s32[]{:S(2)}) async-start(s8[4718592]{0:T(1024)(128)(4,1)} %bitcast.60), calls=%async_computation.1 | async-start | bytes 1048576
  164.8 1.3 copy-start.6

commit v2 on v1

--- a/solution.py
+++ b/solution.py
@@ -15,6 +15,7 @@
 
 EPS = 1e-06
 FRAMES_HERE = 4
+BLOCK = 768
 MESH = pl.DeviceIdType.MESH
 
 
@@ -289,93 +290,217 @@
     )(pay, keep, cols)
 
 
-def back_kernel(res, out, local_sem, send_z, send_y, send_c, recv):
+def back_kernel(
+    res, cols, own, sums, tok, left, part, came, extra,
+    local_sem, send_z, send_y, send_c, recv, own_sem, send_p, recv_p, recv_x,
+):
+    f32, bf16 = jnp.float32, jnp.bfloat16
     me, z, b, y, c = place()
     over_z = [pid((z + dz) % FRAMES_HERE * SPLIT + b) for dz in range(1, FRAMES_HERE)]
     over_y = pid(z * SPLIT + (1 - y) * 2 + c)
     over_c = pid(z * SPLIT + y * 2 + (1 - c))
     greet(over_z + [over_y, over_c])
+    block = BLOCK
     started = []
-
-    def send(src, i, j, sem, peer):
-        copy = remote(src, out.at[i, j], sem, recv.at[i, j], peer)
+    width = res.shape[-1] // 4
+
+    def lanes(t):
+        return pl.ds(t * block, block)
+
+    def send(src, t, i, j, sem, peer):
+        slot = i * FRAMES_HERE + j
+        copy = remote(src, tok.at[slot, :, lanes(t)], sem, recv.at[t, slot], peer)
         copy.start()
         started.append(copy)
 
-    def arrived(i, j, peer):
-        remote(out.at[i, j], out.at[i, j], send_z.at[0], recv.at[i, j], peer).wait_recv()
-
-    local = pltpu.make_async_copy(res.at[z], out.at[b, z], local_sem)
-    local.start()
-    for dz in (2, 1, 3):
-        send(res.at[(z + dz) % FRAMES_HERE], b, z, send_z.at[dz], over_z[dz - 1])
+    def arrived(t, i, j):
+        slot = i * FRAMES_HERE + j
+        place_at = tok.at[slot, :, lanes(t)]
+        remote(place_at, place_at, send_z.at[0, 0], recv.at[t, slot], over_y).wait_recv()
+
+    for t in range(3):
+        for dz in (2, 1, 3):
+            send(
+                res.at[(z + dz) % FRAMES_HERE, :, lanes(t)],
+                t, b, z, send_z.at[t, dz], over_z[dz - 1],
+            )
+    local = [
+        pltpu.make_async_copy(res.at[z], tok.at[b * FRAMES_HERE + z], local_sem.at[0]),
+        pltpu.make_async_copy(cols, left, local_sem.at[1]),
+    ]
+    for copy in local:
+        copy.start()
     order = [0, 1, 3, 2]
-    for dz in order:
-        j = (z + FRAMES_HERE - dz) % FRAMES_HERE
-        if dz:
-            arrived(b, j, over_y)
-        src = out.at[b, j] if dz else res.at[z]
-        send(src, b, j, send_y.at[dz], over_y)
-        send(src, b, j, send_c.at[0, dz], over_c)
-    for dz in order:
-        i, j = (1 - y) * 2 + c, (z + FRAMES_HERE - dz) % FRAMES_HERE
-        arrived(i, j, over_y)
-        send(out.at[i, j], i, j, send_c.at[1, dz], over_c)
-    for yy in range(2):
-        for j in range(FRAMES_HERE):
-            arrived(yy * 2 + (1 - c), j, over_c)
-    local.wait()
+
+    def from_z(t):
+        for dz in order:
+            j = (z + FRAMES_HERE - dz) % FRAMES_HERE
+            if dz:
+                arrived(t, b, j)
+                src = tok.at[b * FRAMES_HERE + j, :, lanes(t)]
+            else:
+                src = res.at[z, :, lanes(t)]
+            send(src, t, b, j, send_y.at[t, dz], over_y)
+            send(src, t, b, j, send_c.at[t, 0, dz], over_c)
+
+    def from_y(t):
+        for dz in order:
+            i, j = (1 - y) * 2 + c, (z + FRAMES_HERE - dz) % FRAMES_HERE
+            arrived(t, i, j)
+            src = tok.at[i * FRAMES_HERE + j, :, lanes(t)]
+            send(src, t, i, j, send_c.at[t, 1, dz], over_c)
+
+    def from_c(t):
+        for yy in range(2):
+            for j in range(FRAMES_HERE):
+                arrived(t, yy * 2 + (1 - c), j)
+
+    low = z < 2
+    end = (z == 0) | (z == 3)
+
+    def at(m):
+        return jnp.where(low, m, 3 - m)
+
+    def block_copy(t, owner, peer_z, to_extra):
+        src = part.at[owner, :, lanes(t)]
+        peer = pid(peer_z * SPLIT + b)
+        if to_extra:
+            return remote(src, extra.at[t], send_p.at[t, 2], recv_x.at[t], peer)
+        return remote(src, came.at[t, z], send_p.at[t, 2], recv_p.at[t, z], peer)
+
+    def near_copy(t, which):
+        owner = jnp.where(end, at(1 + which), at(2 * which))
+        src = part.at[owner, :, lanes(t)]
+        peer = pid(owner * SPLIT + b)
+        return remote(src, came.at[t, z], send_p.at[t, which], recv_p.at[t, z], peer)
+
+    def contract(t):
+        right = tok[:, :, lanes(t)].reshape(SPLIT, FRAMES_HERE * tok.shape[1], block)
+
+        def over_tokens(kind):
+            total = jnp.dot(left[0, kind], right[0], preferred_element_type=f32)
+            for i in range(1, SPLIT):
+                total += jnp.dot(left[i, kind], right[i], preferred_element_type=f32)
+            return total
+
+        product = over_tokens(0)
+        if t == 0:
+            lane = lax.broadcasted_iota(jnp.int32, product.shape, 1)
+            product = jnp.where(lane < width, over_tokens(1), product)
+        rows = part.shape[1]
+        for owner in range(FRAMES_HERE):
+            part[owner, :, t * block : (t + 1) * block] = product[owner * rows : (owner + 1) * rows]
+
+        @pl.when(end)
+        def _():
+            block_copy(t, at(3), at(1), True).start()
+
+        near_copy(t, 1).start()
+        near_copy(t, 0).start()
+
+    def pass_on(t):
+        @pl.when(jnp.logical_not(end))
+        def _():
+            remote(extra.at[t], extra.at[t], send_p.at[t, 2], recv_x.at[t], over_y).wait_recv()
+            far = at(3)
+            part[far, :, t * block : (t + 1) * block] += extra[t]
+            block_copy(t, far, far, False).start()
+
+    from_z(0)
+    from_y(0)
+    from_z(1)
+    for copy in local:
+        copy.wait()
+    from_c(0)
+    contract(0)
+    from_y(1)
+    from_z(2)
+    from_c(1)
+    contract(1)
+    pass_on(0)
+    from_y(2)
+    mine = pltpu.make_async_copy(tok.at[pl.ds(b * FRAMES_HERE, FRAMES_HERE)], own, own_sem)
+    mine.start()
+    from_c(2)
+    contract(2)
+    pass_on(1)
+    pass_on(2)
+
+    def landed(t, src):
+        remote(
+            came.at[t, src], came.at[t, src], send_p.at[t, 0], recv_p.at[t, src], over_y
+        ).wait_recv()
+
+    for t in range(3):
+        here = slice(t * block, (t + 1) * block)
+
+        @pl.when(end)
+        def _():
+            landed(t, at(1))
+            landed(t, at(2))
+            sums[:, here] = part[z, :, here] + came[t, at(1)] + came[t, at(2)]
+
+        @pl.when(jnp.logical_not(end))
+        def _():
+            landed(t, at(0))
+            landed(t, at(2))
+            landed(t, at(3))
+            sums[:, here] = (part[z, :, here] + came[t, at(0)]) + (came[t, at(2)] + came[t, at(3)])
+
+    mine.wait()
     for copy in started:
         copy.wait_send()
-
-
-def send_back(res):
+    for t in range(3):
+        near_copy(t, 0).wait_send()
+        near_copy(t, 1).wait_send()
+
+        @pl.when(end)
+        def _():
+            block_copy(t, at(3), at(1), True).wait_send()
+
+        @pl.when(jnp.logical_not(end))
+        def _():
+            block_copy(t, at(3), at(3), False).wait_send()
+
+
+def send_back(res, cols):
     dma = pltpu.SemaphoreType.DMA
+    frames, rows, wide = res.shape
+    shard = cols.shape[2] // frames
+    f32 = jnp.float32
+    flops = 2 * cols.shape[2] * SPLIT * cols.shape[3] * wide
     return pl.pallas_call(
         back_kernel,
-        out_shape=jax.ShapeDtypeStruct((SPLIT,) + res.shape, res.dtype),
-        in_specs=[pl.BlockSpec(memory_space=pl.ANY)],
-        out_specs=pl.BlockSpec(memory_space=pl.ANY),
-        scratch_shapes=[dma, dma((4,)), dma((4,)), dma((2, 4)), dma((4, 4))],
-        compiler_params=pltpu.CompilerParams(collective_id=2, has_side_effects=True),
-    )(res)
-
-
-def sums_kernel(part, out, local_sem, send_z, recv_z):
-    me, z, b, y, c = place()
-    over_z = [pid((z + dz) % FRAMES_HERE * SPLIT + b) for dz in range(1, FRAMES_HERE)]
-    greet(over_z)
-    local = pltpu.make_async_copy(part.at[z], out.at[z], local_sem)
-    copies = [
-        remote(
-            part.at[(z + dz) % FRAMES_HERE],
-            out.at[z],
-            send_z.at[dz],
-            recv_z.at[dz],
-            over_z[dz - 1],
-        )
-        for dz in (2, 1, 3)
-    ]
-    for copy in copies + [local]:
-        copy.start()
-    for dz in (1, 2, 3):
-        came = (z + FRAMES_HERE - dz) % FRAMES_HERE
-        remote(part.at[z], out.at[came], send_z.at[dz], recv_z.at[dz], over_z[dz - 1]).wait_recv()
-    local.wait()
-    for copy in copies:
-        copy.wait_send()
-
-
-def send_sums(part):
-    dma = pltpu.SemaphoreType.DMA
-    return pl.pallas_call(
-        sums_kernel,
-        out_shape=jax.ShapeDtypeStruct(part.shape, part.dtype),
-        in_specs=[pl.BlockSpec(memory_space=pl.ANY)],
-        out_specs=pl.BlockSpec(memory_space=pl.ANY),
-        scratch_shapes=[dma, dma((4,)), dma((4,))],
-        compiler_params=pltpu.CompilerParams(collective_id=3, has_side_effects=True),
-    )(part)
+        out_shape=[
+            jax.ShapeDtypeStruct(res.shape, res.dtype),
+            jax.ShapeDtypeStruct((shard, wide), f32),
+        ],
+        in_specs=[pl.BlockSpec(memory_space=pl.ANY)] * 2,
+        out_specs=[
+            pl.BlockSpec(memory_space=pl.ANY),
+            pl.BlockSpec(memory_space=pltpu.VMEM),
+        ],
+        scratch_shapes=[
+            pltpu.VMEM((SPLIT * frames, rows, wide), res.dtype),
+            pltpu.VMEM(cols.shape, cols.dtype),
+            pltpu.VMEM((frames, shard, wide), f32),
+            pltpu.VMEM((3, frames, shard, wide // 3), f32),
+            pltpu.VMEM((3, shard, wide // 3), f32),
+            dma((2,)),
+            dma((3, 4)),
+            dma((3, 4)),
+            dma((3, 2, 4)),
+            dma((3, 16)),
+            dma,
+            dma((3, 3)),
+            dma((3, 4)),
+            dma((3,)),
+        ],
+        cost_estimate=pl.CostEstimate(flops=flops, bytes_accessed=4 * res.size, transcendentals=0),
+        compiler_params=pltpu.CompilerParams(
+            collective_id=2, has_side_effects=True, vmem_limit_bytes=40 * 1024 * 1024
+        ),
+    )(res, cols)
 
 
 def attention_kernel(pay, allow, out, dk_sum, dv_sum):
@@ -402,12 +527,12 @@
         )
 
     for f in range(frames):
-        query, d_out = part(0, f), part(3, f)
+        query, d_out = part(1, f), part(0, f)
         scores, dprob = [], []
         for g in range(frames):
-            raw = head_sums(query * part(1, g)) * scale
+            raw = head_sums(query * part(2, g)) * scale
             scores.append(jnp.where(allow[f * frames + g] > 0, raw, -1e30))
-            dprob.append(head_sums(d_out * part(2, g)))
+            dprob.append(head_sums(d_out * part(3, g)))
         top = functools.reduce(jnp.maximum, scores)
         expo = [jnp.exp(s - top) for s in scores]
         total = functools.reduce(jnp.add, expo)
@@ -419,8 +544,8 @@
             pb = jnp.dot(probs[g].astype(bf16), spread, preferred_element_type=f32)
             dscore = (probs[g] * (dprob[g] - inner)).astype(bf16)
             ds = jnp.dot(dscore, spread, preferred_element_type=f32)
-            attn += pb * part(2, g)
-            d_query += ds * part(1, g)
+            attn += pb * part(3, g)
+            d_query += ds * part(2, g)
             if f == 0:
                 dk_sum[g] = ds * query
                 dv_sum[g] = pb * d_out
@@ -454,25 +579,32 @@
     shard, wide_qkv = w_qkv.shape
     wide = wide_qkv + w_out.shape[1]
     rows = band // frames
-    blocks = jnp.concatenate([w_qkv, w_out], 1).reshape(shard, 3, wide // 3).transpose(1, 0, 2)
-    weights = gather_weights(blocks)
-    weights = weights.transpose(1, 2, 0, 3).reshape(model, wide)
-    qkv_full, out_full = weights[:, :wide_qkv], weights[:, wide_qkv:]
+    width = wide // 4
+    blocks = jnp.concatenate([w_out, w_qkv], 1).reshape(shard, 3, BLOCK).transpose(1, 0, 2)
+    gathered = gather_weights(blocks)
+    weights = [gathered[t].reshape(model, BLOCK) for t in range(3)]
 
     tok_float = tokens.astype(f32)
     inv_rms = lax.rsqrt(jnp.mean(tok_float * tok_float, -1, keepdims=True) + EPS)
     normed = tok_float * inv_rms
     hidden = (normed * norm_gain).astype(bf16)
-    qkv = jnp.dot(hidden, qkv_full, preferred_element_type=f32).astype(bf16)
-    d_attn = jnp.dot(cotangent, out_full, preferred_element_type=f32).astype(bf16)
-    pay = jnp.concatenate([qkv, d_attn], 1).reshape(frames, rows, wide)
+    is_attn = jnp.arange(BLOCK) < width
+
+    def project(a, t):
+        return jnp.dot(a, weights[t], preferred_element_type=f32)
+
+    first = jnp.where(is_attn, project(cotangent, 0), project(hidden, 0))
+    pay = jnp.concatenate(
+        [first.astype(bf16), project(hidden, 1).astype(bf16), project(hidden, 2).astype(bf16)], 1
+    ).reshape(frames, rows, wide)
     keep = jnp.repeat(keep_tiles[0].astype(f32), TILE).reshape(frames, 1, rows)
     keep = jnp.pad(jnp.broadcast_to(keep, (frames, 8, rows)), ((0, 0), (0, 0), (0, 128 - rows)))
 
     def owners_columns(a):
-        return a.reshape(band, frames, SPLIT, shard).transpose(2, 0, 1, 3).reshape(SPLIT, band, -1)
-
-    cols = jnp.concatenate([owners_columns(hidden), owners_columns(cotangent)], 2)
+        cut = a.T.reshape(frames, SPLIT, shard, band)
+        return cut.transpose(1, 0, 2, 3).reshape(SPLIT, 1, frames * shard, band)
+
+    cols = jnp.concatenate([owners_columns(hidden), owners_columns(cotangent)], 1)
     pay_at, keep_at, cols_at = send_forward(pay, keep, cols)
 
     frame_block = jnp.arange(frames) // TB
@@ -484,31 +616,23 @@
     allow = jnp.broadcast_to(
         allow.reshape(frames * frames, rows, 1).astype(f32), (frames * frames, rows, 128)
     )
-    res = send_back(attention(pay_at, allow))
-
-    res_all = res.reshape(SPLIT * band, wide)
-    width = wide // 4
-    mine = lax.dynamic_index_in_dim(res, lax.axis_index("tm") % SPLIT, 0, keepdims=False)
-    mine = mine.reshape(band, wide)
-    attn, d_qkv = mine[:, :width], mine[:, width:]
-    cols_all = cols_at.reshape(SPLIT * band, -1)
-    half = cols_all.shape[1] // 2
-    part_qkv = jnp.einsum(
-        "td,te->de", cols_all[:, :half], res_all[:, width:], preferred_element_type=f32
-    )
-    part_out = jnp.einsum(
-        "td,te->de", cols_all[:, half:], res_all[:, :width], preferred_element_type=f32
-    )
-    parts = jnp.concatenate([part_qkv, part_out], 1).reshape(frames, shard, wide)
-    sums = jnp.sum(send_sums(parts), 0)
-    grad_qkv, grad_out = sums[:, :wide_qkv], sums[:, wide_qkv:]
+    own, sums = send_back(attention(pay_at, allow), cols_at)
+    grad_out, grad_qkv = sums[:, :width], sums[:, width:]
+    own = own.reshape(band, wide)
+    results = [own[:, t * BLOCK : (t + 1) * BLOCK] for t in range(3)]
+    zero = jnp.zeros((), bf16)
+
+    def project_back(a, t):
+        return lax.dot_general(a, weights[t], (((1,), (1,)), ((), ())), preferred_element_type=f32)
 
     d_hidden = lax.optimization_barrier(
-        jnp.einsum("te,de->td", d_qkv, qkv_full, preferred_element_type=f32).astype(bf16)
-    )
-    mixed = (
-        tok_float + jnp.einsum("te,de->td", attn, out_full, preferred_element_type=f32)
-    ).astype(bf16)
+        (
+            project_back(jnp.where(is_attn, zero, results[0]), 0)
+            + project_back(results[1], 1)
+            + project_back(results[2], 2)
+        ).astype(bf16)
+    )
+    mixed = (tok_float + project_back(jnp.where(is_attn, results[0], zero), 0)).astype(bf16)
     grad = d_hidden.astype(f32) * norm_gain
     grad_tokens = cotangent.astype(f32) + inv_rms * (
         grad - normed * jnp.mean(grad * normed, -1, keepdims=True)

time: 235 us -> 179 us (0.76)
  the two profiles are of different devices: /device:TPU:16 before, /device:TPU:0 now
where the time goes in v2:
time: 179 us
  Pallas kernels  149 us (83%)
  local copies, waits for them, and re-layouts  14.4 us (8%)
  matrix products  9.28 us (5%)
  other arithmetic  5.22 us (3%)
    pallas_call x1, Pallas kernels, send_back(): pl.pallas_call(back_kernel, out_shape=[jax.ShapeDtypeStruct(res.shape, re...  78.1 us
    pallas_call x1, Pallas kernels, gather_weights(): pl.pallas_call(gather_kernel, out_shape=jax.ShapeDtypeStruct((3, owners)...  35.2 us
    pallas_call x1, Pallas kernels, send_forward(): pl.pallas_call(forward_kernel, out_shape=[jax.ShapeDtypeStruct(a.shape, a...  30.4 us
    dot_general x4, matrix products, project_back(): lax.dot_general(a, weights[t], (((1,), (1,)), ((), ())), preferred_elemen...  5.67 us
    pallas_call x1, Pallas kernels, attention(): pl.pallas_call(attention_kernel, out_shape=jax.ShapeDtypeStruct(pay.shape...  4.99 us
    unnamed x28, local copies, waits for them, and re-layouts  4.37 us
    dot_general x4, matrix products, project(): return jnp.dot(a, weights[t], preferred_element_type=f32)  3.61 us

profile of v2, /device:TPU:0, one launch (start us, length us, event | category | flops | bytes accessed | tf_op | source)
XLA Modules:
  0.0 178.6 jit_solution(7405954470928399953)
XLA Ops:
  0.6 1.2 pad_maximum_fusion.2
  1.8 0.7 copy.36
  2.5 35.2 %shard_map.102 = bf16[3,16,72,768]{3,2,1,0:T(8,128)(2,1)} custom-call(bf16[3,72,768]{2,1,0:T(8,128)(2,1)} %bitcast.104), custom_call_target="tpu_custom_call" | custom-call | tf_op jit(solution)/shard_map/pallas_call | solution.py:225
  37.8 2.9 %fusion.36 = (bf16[1,16,72,768]{3,2,1,0:T(8,128)(2,1)S(1)}, bf16[1,16,72,768]{3,2,1,0:T(8,128)(2,1)S(1)}, bf16[1,16,72,768]{3,2,1,0:T(8,128)(2,1)S(1)}) fusion(bf16[3,16,72,768]{3,2,1,0:T(8,128)(2,1)} %shard_map.102), kind=kLoop, calls=%fused_computation.61 | loop fusion | bytes 10616832 | tf_op jit(solution)/shard_map/slice | solution.py:585
  40.8 0.7 convolution_bitcast_fusion
  41.5 0.7 copy-done.2
  42.5 1.0 fusion.8
  43.5 0.9 convolution_convert_fusion
  44.5 0.9 convolution_convert_fusion.1
  45.5 1.7 copy.22
  48.0 1.1 pad_maximum_fusion.1.cols
  50.0 30.4 %shard_map.103 = (bf16[4,64,2304]{2,1,0:T(8,128)(2,1)}, f32[4,8,128]{2,1,0:T(8,128)}, bf16[4,2,288,256]{3,2,1,0:T(8,128)(2,1)}) custom-call(bf16[4,64,2304]{2,1,0:T(8,128)(2,1)} %bitcast.98, f32[4,8,128]{2,1,0:T(8,128)} %pad.4.keep, bf16[4,2,288,256]{3,2,1,0:T(8,128)(2,1)} %pad_maximum_fusion.1.cols), custom_call_target="tpu_custom_call" | custom-call | tf_op jit(solution)/shard_map/pallas_call | solution.py:283
  80.5 0.7 slice_compare_fusion
  82.1 1.3 copy-done
  83.4 5.0 %shard_map.104.res = bf16[4,64,2304]{2,1,0:T(8,128)(2,1)S(1)} custom-call(bf16[4,64,2304]{2,1,0:T(8,128)(2,1)S(1)} %copy-done, f32[16,64,128]{2,1,0:T(8,128)S(1)} %broadcast_in_dim.62.allow), custom_call_target="tpu_custom_call" | custom-call | tf_op jit(solution)/shard_map/pallas_call | solution.py:564
  88.4 78.1 %shard_map.105 = (bf16[4,64,2304]{2,1,0:T(8,128)(2,1)S(1)}, f32[72,2304]{1,0:T(8,128)S(1)}) custom-call(bf16[4,64,2304]{2,1,0:T(8,128)(2,1)S(1)} %shard_map.104.res, bf16[4,2,288,256]{3,2,1,0:T(8,128)(2,1)S(1)} %copy-done.1), custom_call_target="tpu_custom_call" | custom-call | flops 1358954496 | bytes 2359296 | tf_op jit(solution)/shard_map/pallas_call | solution.py:472
  166.5 0.8 slice.36
  167.2 1.2 copy.32
  168.4 2.5 %fusion.24 = f32[256,1152]{1,0:T(8,128)S(1)} fusion(bf16[1152,768]{1,0:T(8,128)(2,1)} %bitcast.92, bf16[256,768]{0,1:T(8,128)(2,1)S(1)} %copy.32, pred[768]{0:T(1024)(128)(4,1)S(1)} %iota_compare_fusion), kind=kOutput, calls=%fused_computation.36 | convolution fusion | flops 453181440 | bytes 3343104 | tf_op jit(solution)/shard_map/dot_general | solution.py:626
  171.6 0.7 copy-done.8
  172.4 0.7 fusion.1
  173.5 1.2 fusion.19
  175.1 1.7 fusion.2
  176.9 1.0 slice.34
  (59 shorter events, 5.0 us)
Async XLA Ops:
  37.8 3.0 %copy-start.9 = (bf16[1,256,1152]{2,1,0:T(8,128)(2,1)S(1)}, bf16[1,256,1152]{2,1,0:T(8,128)(2,1)}, u32[]{:S(2)}) copy-start(bf16[1,256,1152]{2,1,0:T(8,128)(2,1)} %param.13) | copy-start | bytes 1769476
  40.7 1.8 copy-start.3
  40.7 2.8 %copy-start.7 = (bf16[1,16,72,768]{3,2,1,0:T(8,128)(2,1)}, bf16[1,16,72,768]{3,2,1,0:T(8,128)(2,1)S(1)}, u32[]{:S(2)}) copy-start(bf16[1,16,72,768]{3,2,1,0:T(8,128)(2,1)S(1)} %get-tuple-element.15) | copy-start | bytes 5308420
  40.7 3.7 %copy-start.5 = (bf16[1,16,72,768]{3,2,1,0:T(8,128)(2,1)}, bf16[1,16,72,768]{3,2,1,0:T(8,128)(2,1)S(1)}, u32[]{:S(2)}) copy-start(bf16[1,16,72,768]{3,2,1,0:T(8,128)(2,1)S(1)} %get-tuple-element.14) | copy-start | bytes 5308420
  40.8 1.5 copy-start.2
  40.8 1.7 copy-start.10
  48.0 1.1 copy-start.12
  50.0 31.4 %copy-start.11 = (s32[1,2,2]{2,1,0:T(2,128)S(1)}, s32[1,2,2]{2,1,0:T(2,128)}, u32[]{:S(2)}) copy-start(s32[1,2,2]{2,1,0:T(2,128)} %param.11) | copy-start | bytes 52
  82.1 1.3 copy-start
  83.4 5.0 %copy-start.1 = (bf16[4,2,288,256]{3,2,1,0:T(8,128)(2,1)S(1)}, bf16[4,2,288,256]{3,2,1,0:T(8,128)(2,1)}, u32[]{:S(2)}) copy-start(bf16[4,2,288,256]{3,2,1,0:T(8,128)(2,1)} %get-tuple-element.11.cols) | copy-start | bytes 3538948
  168.4 2.5 %copy-start.6 = (bf16[1,16,72,768]{3,2,1,0:T(8,128)(2,1)S(1)}, bf16[1,16,72,768]{3,2,1,0:T(8,128)(2,1)}, u32[]{:S(2)}) copy-start(bf16[1,16,72,768]{3,2,1,0:T(8,128)(2,1)} %copy-done.5) | copy-start | bytes 5308420
  170.9 1.5 copy-start.8
  173.5 1.7 copy-start.4

commit v3 on v2

--- a/solution.py
+++ b/solution.py
@@ -157,137 +157,216 @@
     )
 
 
-def gather_kernel(w_ref, out_ref, local_sem, send_z, send_y, send_x, send_c, recv):
+def forward_kernel(
+    w_ref, cols, keep, w_out, pay_out, keep_out, cols_out, held, left, pay,
+    local_sem, send_z, send_y, send_x, send_c, recv, save_sem,
+    send_k, recv_k, send_b, recv_b, send_p, recv_p, own_sem,
+):
+    f32 = jnp.float32
     x = lax.axis_index("groups")
     me, z, b, y, c = place()
     over_z = [pid((z + dz) % FRAMES_HERE * SPLIT + b) for dz in range(1, FRAMES_HERE)]
+    over_b = [pid(z * SPLIT + (b + db) % SPLIT) for db in range(1, SPLIT)]
     over_y = pid(z * SPLIT + (1 - y) * 2 + c)
     over_c = pid(z * SPLIT + y * 2 + (1 - c))
     over_x = {"groups": 1 - x}
-    greet(over_z + [over_y, over_c, over_x])
-    mine = (x, 2)
+    greet(over_z + over_b + [over_x])
+    blocks = (2, x, 1 - x)
     started = []
 
-    def send(src, t, k, sem, peer):
-        copy = remote(src, out_ref.at[t, k], sem, recv.at[t, k], peer)
+    def start(copy):
         copy.start()
         started.append(copy)
 
-    def arrived(t, k, peer):
-        remote(out_ref.at[t, k], out_ref.at[t, k], send_z.at[0, 0], recv.at[t, k], peer).wait_recv()
+    def send(src, t, k, sem, peer):
+        start(remote(src, held.at[t, k], sem, recv.at[t, k], peer))
+
+    def arrived(t, k):
+        remote(held.at[t, k], held.at[t, k], send_z.at[0, 0], recv.at[t, k], over_y).wait_recv()
 
     local = [
-        pltpu.make_async_copy(w_ref.at[t], out_ref.at[t, me], local_sem.at[i])
-        for i, t in enumerate(mine)
+        pltpu.make_async_copy(w_ref.at[2], held.at[2, me], local_sem.at[0]),
+        pltpu.make_async_copy(w_ref.at[x], held.at[x, me], local_sem.at[1]),
+        pltpu.make_async_copy(cols, left, local_sem.at[2]),
+        pltpu.make_async_copy(keep.at[z], keep_out.at[z], local_sem.at[3]),
+        pltpu.make_async_copy(cols.at[b], cols_out.at[b], local_sem.at[4]),
     ]
     for copy in local:
         copy.start()
-    for dz in range(1, FRAMES_HERE):
-        for i, t in enumerate(mine):
-            send(w_ref.at[t], t, me, send_z.at[i, dz], over_z[dz - 1])
+    for i in range(2):
+        for dz in (2, 1, 3):
+            send(w_ref.at[blocks[i]], blocks[i], me, send_z.at[i, dz], over_z[dz - 1])
     shards = [(z + FRAMES_HERE - dz) % FRAMES_HERE * SPLIT for dz in range(FRAMES_HERE)]
     order = [0, 1, 3, 2]
-    for dz in order:
-        k = shards[dz] + b
-        for i, t in enumerate(mine):
+
+    def from_z(i):
+        t = blocks[i]
+        for dz in order:
+            k = shards[dz] + b
             if dz:
-                arrived(t, k, over_y)
-            src = out_ref.at[t, k] if dz else w_ref.at[t]
+                arrived(t, k)
+            src = held.at[t, k] if dz else w_ref.at[t]
             send(src, t, k, send_y.at[i, dz], over_y)
-            if i == 0:
+            if i == 1:
                 send(src, t, k, send_x.at[0, dz], over_x)
             send(src, t, k, send_c.at[i, 0, dz], over_c)
-    for dz in order:
-        k = shards[dz] + (1 - y) * 2 + c
-        for i, t in enumerate(mine):
-            arrived(t, k, over_y)
-            if i == 0:
-                send(out_ref.at[t, k], t, k, send_x.at[1, dz], over_x)
-            send(out_ref.at[t, k], t, k, send_c.at[i, 1, dz], over_c)
-    for j in range(2):
+
+    def from_y(i):
+        t = blocks[i]
+        for dz in order:
+            k = shards[dz] + (1 - y) * 2 + c
+            arrived(t, k)
+            if i == 1:
+                send(held.at[t, k], t, k, send_x.at[1, dz], over_x)
+            send(held.at[t, k], t, k, send_c.at[i, 1, dz], over_c)
+
+    def from_x(j):
+        t = blocks[2]
         for dz in order:
             k = shards[dz] + (y if j == 0 else 1 - y) * 2 + c
-            arrived(1 - x, k, over_x)
-            send(out_ref.at[1 - x, k], 1 - x, k, send_c.at[2, j, dz], over_c)
-    for t in range(3):
+            arrived(t, k)
+            send(held.at[t, k], t, k, send_c.at[2, j, dz], over_c)
+
+    rows = pay.shape[2]
+    width = 3 * BLOCK // 4
+    own = []
+
+    def project(i):
+        t = blocks[i]
         for yy in range(2):
             for zz in range(FRAMES_HERE):
-                arrived(t, zz * SPLIT + yy * 2 + (1 - c), over_c)
+                arrived(t, zz * SPLIT + yy * 2 + (1 - c))
+        save = pltpu.make_async_copy(held.at[t], w_out.at[t], save_sem.at[i])
+        save.start()
+        own.append(save)
+
+        def over_shards(kind):
+            total = None
+            for k in range(FRAMES_HERE * SPLIT):
+                term = lax.dot_general(
+                    left[k % SPLIT, kind, k // SPLIT],
+                    held[t, k],
+                    (((0,), (0,)), ((), ())),
+                    preferred_element_type=f32,
+                )
+                total = term if total is None else total + term
+            return total
+
+        def store(value):
+            value = value.astype(pay.dtype)
+            for to in range(FRAMES_HERE):
+                pay[t, to] = value[to * rows : (to + 1) * rows]
+
+        if i == 0:
+            store(over_shards(0))
+        else:
+
+            @pl.when(t != 0)
+            def _():
+                store(over_shards(0))
+
+            @pl.when(t == 0)
+            def _():
+                value = over_shards(0)
+                lane = lax.broadcasted_iota(jnp.int32, value.shape, 1)
+                store(jnp.where(lane < width, over_shards(1), value))
+
+        lanes = pl.ds(pl.multiple_of(t * BLOCK, BLOCK), BLOCK)
+        for dz in (2, 1, 3):
+            start(
+                remote(
+                    pay.at[t, (z + dz) % FRAMES_HERE],
+                    pay_out.at[z, :, lanes],
+                    send_p.at[i, dz],
+                    recv_p.at[i, dz],
+                    over_z[dz - 1],
+                )
+            )
+        keep_own = pltpu.make_async_copy(pay.at[t, z], pay_out.at[z, :, lanes], own_sem.at[i])
+        keep_own.start()
+        own.append(keep_own)
+
+    from_z(0)
+    from_y(0)
+    from_z(1)
     for copy in local:
+        copy.wait()
+    project(0)
+    from_y(1)
+    from_x(0)
+    for dz in (2, 1, 3):
+        to = (z + dz) % FRAMES_HERE
+        start(
+            remote(keep.at[to], keep_out.at[z], send_k.at[dz], recv_k.at[dz], over_z[dz - 1])
+        )
+    for db in (2, 1, 3):
+        to = (b + db) % SPLIT
+        start(remote(cols.at[to], cols_out.at[b], send_b.at[db], recv_b.at[db], over_b[db - 1]))
+    project(1)
+    from_x(1)
+    project(2)
+    for dz in (1, 2, 3):
+        came = (z + FRAMES_HERE - dz) % FRAMES_HERE
+        peer = over_z[dz - 1]
+        remote(keep.at[z], keep_out.at[came], send_k.at[dz], recv_k.at[dz], peer).wait_recv()
+        for i in range(3):
+            lanes = pl.ds(pl.multiple_of(blocks[i] * BLOCK, BLOCK), BLOCK)
+            remote(
+                pay.at[blocks[i], z],
+                pay_out.at[came, :, lanes],
+                send_p.at[i, dz],
+                recv_p.at[i, dz],
+                peer,
+            ).wait_recv()
+    for db in (1, 2, 3):
+        came = (b + SPLIT - db) % SPLIT
+        remote(cols.at[b], cols_out.at[came], send_b.at[db], recv_b.at[db], over_b[db - 1]).wait_recv()
+    for copy in own:
         copy.wait()
     for copy in started:
         copy.wait_send()
 
 
-def gather_weights(blocks):
+def forward(blocks, cols, keep):
     owners = FRAMES_HERE * SPLIT
     dma = pltpu.SemaphoreType.DMA
-    return pl.pallas_call(
-        gather_kernel,
-        out_shape=jax.ShapeDtypeStruct((3, owners) + blocks.shape[1:], blocks.dtype),
-        in_specs=[pl.BlockSpec(memory_space=pl.ANY)],
-        out_specs=pl.BlockSpec(memory_space=pl.ANY),
-        scratch_shapes=[
-            dma((2,)),
-            dma((2, FRAMES_HERE)),
-            dma((2, FRAMES_HERE)),
-            dma((2, FRAMES_HERE)),
-            dma((3, 2, FRAMES_HERE)),
-            dma((3, owners)),
-        ],
-        compiler_params=pltpu.CompilerParams(collective_id=0, has_side_effects=True),
-    )(blocks)
-
-
-def forward_kernel(
-    pay, keep, cols, pay_out, keep_out, cols_out, local_sem, send_z, recv_z, send_b, recv_b
-):
-    me, z, b, y, c = place()
-    over_z = [pid((z + dz) % FRAMES_HERE * SPLIT + b) for dz in range(1, FRAMES_HERE)]
-    over_b = [pid(z * SPLIT + (b + db) % SPLIT) for db in range(1, SPLIT)]
-    greet(over_z + over_b)
-    local = [
-        pltpu.make_async_copy(pay.at[z], pay_out.at[z], local_sem.at[0]),
-        pltpu.make_async_copy(keep.at[z], keep_out.at[z], local_sem.at[1]),
-        pltpu.make_async_copy(cols.at[b], cols_out.at[b], local_sem.at[2]),
-    ]
-    copies = []
-    for dz in (2, 1, 3):
-        to = (z + dz) % FRAMES_HERE
-        peer = over_z[dz - 1]
-        copies.append(remote(keep.at[to], keep_out.at[z], send_z.at[1, dz], recv_z.at[1, dz], peer))
-        copies.append(remote(pay.at[to], pay_out.at[z], send_z.at[0, dz], recv_z.at[0, dz], peer))
-    for db in (2, 1, 3):
-        to = (b + db) % SPLIT
-        copies.append(
-            remote(cols.at[to], cols_out.at[b], send_b.at[db], recv_b.at[db], over_b[db - 1])
-        )
-    for copy in copies + local:
-        copy.start()
-    for dz in (1, 2, 3):
-        came = (z + FRAMES_HERE - dz) % FRAMES_HERE
-        peer = over_z[dz - 1]
-        remote(keep.at[z], keep_out.at[came], send_z.at[1, dz], recv_z.at[1, dz], peer).wait_recv()
-        remote(pay.at[z], pay_out.at[came], send_z.at[0, dz], recv_z.at[0, dz], peer).wait_recv()
-    for db in (1, 2, 3):
-        came = (b + SPLIT - db) % SPLIT
-        remote(cols.at[b], cols_out.at[came], send_b.at[db], recv_b.at[db], over_b[db - 1]).wait_recv()
-    for copy in local:
-        copy.wait()
-    for copy in copies:
-        copy.wait_send()
-
-
-def send_forward(pay, keep, cols):
-    dma = pltpu.SemaphoreType.DMA
+    shard = blocks.shape[1]
+    rows = cols.shape[-1] // FRAMES_HERE
+    held = (3, owners, shard, BLOCK)
+    pay = (FRAMES_HERE, rows, 3 * BLOCK)
     return pl.pallas_call(
         forward_kernel,
-        out_shape=[jax.ShapeDtypeStruct(a.shape, a.dtype) for a in (pay, keep, cols)],
+        out_shape=[
+            jax.ShapeDtypeStruct(held, blocks.dtype),
+            jax.ShapeDtypeStruct(pay, blocks.dtype),
+            jax.ShapeDtypeStruct(keep.shape, keep.dtype),
+            jax.ShapeDtypeStruct(cols.shape, cols.dtype),
+        ],
         in_specs=[pl.BlockSpec(memory_space=pl.ANY)] * 3,
-        out_specs=[pl.BlockSpec(memory_space=pl.ANY)] * 3,
-        scratch_shapes=[dma((3,)), dma((2, 4)), dma((2, 4)), dma((4,)), dma((4,))],
-        compiler_params=pltpu.CompilerParams(collective_id=1, has_side_effects=True),
-    )(pay, keep, cols)
+        out_specs=[pl.BlockSpec(memory_space=pl.ANY)] * 4,
+        scratch_shapes=[
+            pltpu.VMEM(held, blocks.dtype),
+            pltpu.VMEM(cols.shape, cols.dtype),
+            pltpu.VMEM((3, FRAMES_HERE, rows, BLOCK), blocks.dtype),
+            dma((5,)),
+            dma((2, 4)),
+            dma((2, 4)),
+            dma((2, 4)),
+            dma((3, 2, 4)),
+            dma((3, owners)),
+            dma((3,)),
+            dma((4,)),
+            dma((4,)),
+            dma((4,)),
+            dma((4,)),
+            dma((3, 4)),
+            dma((3, 4)),
+            dma((3,)),
+        ],
+        compiler_params=pltpu.CompilerParams(
+            collective_id=0, has_side_effects=True, vmem_limit_bytes=40 * 1024 * 1024
+        ),
+    )(blocks, cols, keep)
 
 
 def back_kernel(
@@ -581,31 +660,22 @@
     rows = band // frames
     width = wide // 4
     blocks = jnp.concatenate([w_out, w_qkv], 1).reshape(shard, 3, BLOCK).transpose(1, 0, 2)
-    gathered = gather_weights(blocks)
-    weights = [gathered[t].reshape(model, BLOCK) for t in range(3)]
-
     tok_float = tokens.astype(f32)
     inv_rms = lax.rsqrt(jnp.mean(tok_float * tok_float, -1, keepdims=True) + EPS)
     normed = tok_float * inv_rms
     hidden = (normed * norm_gain).astype(bf16)
     is_attn = jnp.arange(BLOCK) < width
-
-    def project(a, t):
-        return jnp.dot(a, weights[t], preferred_element_type=f32)
-
-    first = jnp.where(is_attn, project(cotangent, 0), project(hidden, 0))
-    pay = jnp.concatenate(
-        [first.astype(bf16), project(hidden, 1).astype(bf16), project(hidden, 2).astype(bf16)], 1
-    ).reshape(frames, rows, wide)
     keep = jnp.repeat(keep_tiles[0].astype(f32), TILE).reshape(frames, 1, rows)
     keep = jnp.pad(jnp.broadcast_to(keep, (frames, 8, rows)), ((0, 0), (0, 0), (0, 128 - rows)))
 
     def owners_columns(a):
         cut = a.T.reshape(frames, SPLIT, shard, band)
-        return cut.transpose(1, 0, 2, 3).reshape(SPLIT, 1, frames * shard, band)
+        return cut.transpose(1, 0, 2, 3)[:, None]
 
     cols = jnp.concatenate([owners_columns(hidden), owners_columns(cotangent)], 1)
-    pay_at, keep_at, cols_at = send_forward(pay, keep, cols)
+    gathered, pay_at, keep_at, cols_at = forward(blocks, cols, keep)
+    weights = [gathered[t].reshape(model, BLOCK) for t in range(3)]
+    cols_at = cols_at.reshape(SPLIT, 2, frames * shard, band)
 
     frame_block = jnp.arange(frames) // TB
     same_block = frame_block[:, None] == frame_block[None, :]

time: 179 us -> 156 us (0.87)
  Pallas kernels: 149 us -> 138 us
  local copies, waits for them, and re-layouts: 14.4 us -> 8.69 us
  matrix products: 9.28 us -> 3.72 us
    pallas_call x2 -> x1, Pallas kernels: 65.6 us -> 58.3 us  [forward(): pl.pallas_call(forward_kernel, out_shape=[jax.ShapeDtypeStruct(held, bloc...]
    pallas_call x1, Pallas kernels: 78.1 us -> 74.3 us  [send_back(): pl.pallas_call(back_kernel, out_shape=[jax.ShapeDtypeStruct(res.shape, re...]
    dot_general x4 -> x0, matrix products: 3.61 us -> none  [project(): return jnp.dot(a, weights[t], preferred_element_type=f32)]
    slice x1, local copies, waits for them, and re-layouts: 2.95 us -> 0.34 us  [four_frames(): weights = [gathered[t].reshape(model, BLOCK) for t in range(3)]]
    dot_general x4, matrix products: 5.67 us -> 3.72 us  [project_back(): lax.dot_general(a, weights[t], (((1,), (1,)), ((), ())), preferred_elemen...]
    unnamed x28 -> x23, local copies, waits for them, and re-layouts: 4.37 us -> 5.08 us
where the time goes in v3:
time: 156 us
  Pallas kernels  138 us (88%)
  local copies, waits for them, and re-layouts  8.69 us (6%)
  other arithmetic  4.6 us (3%)
  matrix products  3.72 us (2%)
    pallas_call x1, Pallas kernels, send_back(): pl.pallas_call(back_kernel, out_shape=[jax.ShapeDtypeStruct(res.shape, re...  74.3 us
    pallas_call x1, Pallas kernels, forward(): pl.pallas_call(forward_kernel, out_shape=[jax.ShapeDtypeStruct(held, bloc...  58.3 us
    pallas_call x1, Pallas kernels, attention(): pl.pallas_call(attention_kernel, out_shape=jax.ShapeDtypeStruct(pay.shape...  5.22 us
    unnamed x23, local copies, waits for them, and re-layouts  5.08 us
    dot_general x4, matrix products, project_back(): lax.dot_general(a, weights[t], (((1,), (1,)), ((), ())), preferred_elemen...  3.72 us

profile of v3, /device:TPU:0, one launch (start us, length us, event | category | flops | bytes accessed | tf_op | source)
XLA Modules:
  0.0 155.7 jit_solution(11481075119967688581)
XLA Ops:
  0.6 1.3 fusion.12
  1.9 1.3 fusion.14
  3.2 0.2 copy.12
  3.5 0.3 copy.14
  3.9 0.1 pad_maximum_fusion.cols
  4.0 0.8 copy-done.6
  4.9 0.1 pad_maximum_fusion.1
  5.1 0.5 copy-done.10
  5.8 58.3 %shard_map.102 = (bf16[3,16,72,768]{3,2,1,0:T(8,128)(2,1)S(1)}, bf16[4,64,2304]{2,1,0:T(8,128)(2,1)S(1)}, f32[4,8,128]{2,1,0:T(8,128)S(1)}, bf16[4,2,4,72,256]{4,3,2,1,0:T(8,128)(2,1)S(1)}) custom-call(bf16[3,72,768]{2,1,0:T(8,128)(2,1)S(1)} %bitcast.51, bf16[4,2,4,72,256]{4,3,2,1,0:T(8,128)(2,1)S(1)} %pad_maximum_fusion.cols, f32[4,8,128]{2,1,0:T(8,128)S(1)} %pad.4.keep), custom_call_target="tpu_custom_call" | custom-call | tf_op jit(solution)/shard_map/pallas_call | solution.py:337
  64.2 2.3 %copy-done = bf16[3,16,72,768]{3,2,1,0:T(8,128)(2,1)} copy-done((bf16[3,16,72,768]{3,2,1,0:T(8,128)(2,1)}, bf16[3,16,72,768]{3,2,1,0:T(8,128)(2,1)S(1)}, u32[]{:S(2)}) %copy-start) | copy-done | bytes 5308440
  66.5 1.1 copy-done.2
  68.2 0.2 broadcast_in_dim.66.allow
  68.4 5.2 %shard_map.103.res = bf16[4,64,2304]{2,1,0:T(8,128)(2,1)S(1)} custom-call(bf16[4,64,2304]{2,1,0:T(8,128)(2,1)S(1)} %get-tuple-element.10.pay, f32[16,64,128]{2,1,0:T(8,128)S(1)} %broadcast_in_dim.66.allow), custom_call_target="tpu_custom_call" | custom-call | tf_op jit(solution)/shard_map/pallas_call | solution.py:643
  73.7 74.3 %shard_map.104 = (bf16[4,64,2304]{2,1,0:T(8,128)(2,1)S(1)}, f32[72,2304]{1,0:T(8,128)S(1)}) custom-call(bf16[4,64,2304]{2,1,0:T(8,128)(2,1)S(1)} %shard_map.103.res, bf16[4,2,288,256]{3,2,1,0:T(8,128)(2,1)S(1)} %bitcast.56), custom_call_target="tpu_custom_call" | custom-call | flops 1358954496 | bytes 2359296 | tf_op jit(solution)/shard_map/pallas_call | solution.py:551
  148.0 0.3 fusion.28
  148.3 0.7 fusion.17
  149.1 0.7 convolution_add_fusion.1
  149.8 0.7 fusion.1
  150.6 0.3 copy-done.4
  150.9 0.4 fusion.7
  151.2 1.3 fusion.13
  152.5 1.5 fusion.2
  154.0 1.0 slice.34
  155.0 0.7 slice.35
  (45 shorter events, 1.2 us)
Async XLA Ops:
  1.9 1.6 %copy-start.5 = (bf16[1,256,1152]{2,1,0:T(8,128)(2,1)S(1)}, bf16[1,256,1152]{2,1,0:T(8,128)(2,1)}, u32[]{:S(2)}) copy-start(bf16[1,256,1152]{2,1,0:T(8,128)(2,1)} %param.13) | copy-start | bytes 1769476
  3.9 1.0 copy-start.6
  3.9 1.0 copy-start.7
  4.9 0.7 copy-start.10
  5.0 62.8 %copy-start.9 = (s32[1,2,2]{2,1,0:T(2,128)S(1)}, s32[1,2,2]{2,1,0:T(2,128)}, u32[]{:S(2)}) copy-start(s32[1,2,2]{2,1,0:T(2,128)} %param.11) | copy-start | bytes 52
  64.2 2.3 %copy-start = (bf16[3,16,72,768]{3,2,1,0:T(8,128)(2,1)}, bf16[3,16,72,768]{3,2,1,0:T(8,128)(2,1)S(1)}, u32[]{:S(2)}) copy-start(bf16[3,16,72,768]{3,2,1,0:T(8,128)(2,1)S(1)} %get-tuple-element.14) | copy-start | bytes 15925252
  66.5 1.1 copy-start.2
  68.2 5.4 %copy-start.3 = (bf16[4,2,4,72,256]{4,3,2,1,0:T(8,128)(2,1)S(1)}, bf16[4,2,4,72,256]{4,3,2,1,0:T(8,128)(2,1)}, u32[]{:S(2)}) copy-start(bf16[4,2,4,72,256]{4,3,2,1,0:T(8,128)(2,1)} %copy-done.2) | copy-start | bytes 3538948
  68.4 79.6 %copy-start.1 = (bf16[3,16,72,768]{3,2,1,0:T(8,128)(2,1)S(1)}, bf16[3,16,72,768]{3,2,1,0:T(8,128)(2,1)}, u32[]{:S(2)}) copy-start(bf16[3,16,72,768]{3,2,1,0:T(8,128)(2,1)} %copy-done) | copy-start | bytes 15925252
  149.8 1.1 copy-start.4
  149.8 1.1 copy-start.8

commit v4 on v3

--- a/solution.py
+++ b/solution.py
@@ -379,7 +379,7 @@
     over_y = pid(z * SPLIT + (1 - y) * 2 + c)
     over_c = pid(z * SPLIT + y * 2 + (1 - c))
     greet(over_z + [over_y, over_c])
-    block = BLOCK
+    block = BLOCK // 2
     started = []
     width = res.shape[-1] // 4
 
@@ -397,7 +397,7 @@
         place_at = tok.at[slot, :, lanes(t)]
         remote(place_at, place_at, send_z.at[0, 0], recv.at[t, slot], over_y).wait_recv()
 
-    for t in range(3):
+    for t in range(6):
         for dz in (2, 1, 3):
             send(
                 res.at[(z + dz) % FRAMES_HERE, :, lanes(t)],
@@ -462,10 +462,10 @@
                 total += jnp.dot(left[i, kind], right[i], preferred_element_type=f32)
             return total
 
-        product = over_tokens(0)
-        if t == 0:
+        product = over_tokens(1 if (t + 1) * block <= width else 0)
+        if t * block < width < (t + 1) * block:
             lane = lax.broadcasted_iota(jnp.int32, product.shape, 1)
-            product = jnp.where(lane < width, over_tokens(1), product)
+            product = jnp.where(lane < width - t * block, over_tokens(1), product)
         rows = part.shape[1]
         for owner in range(FRAMES_HERE):
             part[owner, :, t * block : (t + 1) * block] = product[owner * rows : (owner + 1) * rows]
@@ -490,27 +490,26 @@
     from_z(1)
     for copy in local:
         copy.wait()
-    from_c(0)
-    contract(0)
-    from_y(1)
-    from_z(2)
-    from_c(1)
-    contract(1)
-    pass_on(0)
-    from_y(2)
     mine = pltpu.make_async_copy(tok.at[pl.ds(b * FRAMES_HERE, FRAMES_HERE)], own, own_sem)
-    mine.start()
-    from_c(2)
-    contract(2)
-    pass_on(1)
-    pass_on(2)
+    for t in range(6):
+        from_c(t)
+        contract(t)
+        if t < 5:
+            from_y(t + 1)
+        if t < 4:
+            from_z(t + 2)
+        if t == 4:
+            mine.start()
+        if t > 0:
+            pass_on(t - 1)
+    pass_on(5)
 
     def landed(t, src):
         remote(
             came.at[t, src], came.at[t, src], send_p.at[t, 0], recv_p.at[t, src], over_y
         ).wait_recv()
 
-    for t in range(3):
+    for t in range(6):
         here = slice(t * block, (t + 1) * block)
 
         @pl.when(end)
@@ -529,7 +528,7 @@
     mine.wait()
     for copy in started:
         copy.wait_send()
-    for t in range(3):
+    for t in range(6):
         near_copy(t, 0).wait_send()
         near_copy(t, 1).wait_send()
 
@@ -563,17 +562,17 @@
             pltpu.VMEM((SPLIT * frames, rows, wide), res.dtype),
             pltpu.VMEM(cols.shape, cols.dtype),
             pltpu.VMEM((frames, shard, wide), f32),
-            pltpu.VMEM((3, frames, shard, wide // 3), f32),
-            pltpu.VMEM((3, shard, wide // 3), f32),
+            pltpu.VMEM((6, frames, shard, wide // 6), f32),
+            pltpu.VMEM((6, shard, wide // 6), f32),
             dma((2,)),
-            dma((3, 4)),
-            dma((3, 4)),
-            dma((3, 2, 4)),
-            dma((3, 16)),
+            dma((6, 4)),
+            dma((6, 4)),
+            dma((6, 2, 4)),
+            dma((6, 16)),
             dma,
-            dma((3, 3)),
-            dma((3, 4)),
-            dma((3,)),
+            dma((6, 3)),
+            dma((6, 4)),
+            dma((6,)),
         ],
         cost_estimate=pl.CostEstimate(flops=flops, bytes_accessed=4 * res.size, transcendentals=0),
         compiler_params=pltpu.CompilerParams(

time: 156 us -> 157 us (level)
  no operation moved by 1% of the time
where the time goes in v4:
time: 157 us
  Pallas kernels  139 us (89%)
  local copies, waits for them, and re-layouts  8.69 us (6%)
  other arithmetic  4.6 us (3%)
  matrix products  3.71 us (2%)
    pallas_call x1, Pallas kernels, send_back(): pl.pallas_call(back_kernel, out_shape=[jax.ShapeDtypeStruct(res.shape, re...  75.4 us
    pallas_call x1, Pallas kernels, forward(): pl.pallas_call(forward_kernel, out_shape=[jax.ShapeDtypeStruct(held, bloc...  58.3 us
    pallas_call x1, Pallas kernels, attention(): pl.pallas_call(attention_kernel, out_shape=jax.ShapeDtypeStruct(pay.shape...  5.22 us
    unnamed x23, local copies, waits for them, and re-layouts  5.09 us
    dot_general x4, matrix products, project_back(): lax.dot_general(a, weights[t], (((1,), (1,)), ((), ())), preferred_elemen...  3.71 us

profile of v4, /device:TPU:0, one launch (start us, length us, event | category | flops | bytes accessed | tf_op | source)
XLA Modules:
  0.0 156.8 jit_solution(7920411194236315312)
XLA Ops:
  0.6 1.3 fusion.12
  1.9 1.3 fusion.14
  3.2 0.2 copy.12
  3.5 0.3 copy.14
  3.9 0.1 pad_maximum_fusion.cols
  4.0 0.8 copy-done.6
  4.9 0.1 pad_maximum_fusion.1
  5.1 0.5 copy-done.10
  5.8 58.3 %shard_map.102 = (bf16[3,16,72,768]{3,2,1,0:T(8,128)(2,1)S(1)}, bf16[4,64,2304]{2,1,0:T(8,128)(2,1)S(1)}, f32[4,8,128]{2,1,0:T(8,128)S(1)}, bf16[4,2,4,72,256]{4,3,2,1,0:T(8,128)(2,1)S(1)}) custom-call(bf16[3,72,768]{2,1,0:T(8,128)(2,1)S(1)} %bitcast.51, bf16[4,2,4,72,256]{4,3,2,1,0:T(8,128)(2,1)S(1)} %pad_maximum_fusion.cols, f32[4,8,128]{2,1,0:T(8,128)S(1)} %pad.4.keep), custom_call_target="tpu_custom_call" | custom-call | tf_op jit(solution)/shard_map/pallas_call | solution.py:337
  64.2 2.3 %copy-done = bf16[3,16,72,768]{3,2,1,0:T(8,128)(2,1)} copy-done((bf16[3,16,72,768]{3,2,1,0:T(8,128)(2,1)}, bf16[3,16,72,768]{3,2,1,0:T(8,128)(2,1)S(1)}, u32[]{:S(2)}) %copy-start) | copy-done | bytes 5308440
  66.5 1.1 copy-done.2
  68.2 0.2 broadcast_in_dim.66.allow
  68.4 5.2 %shard_map.103.res = bf16[4,64,2304]{2,1,0:T(8,128)(2,1)S(1)} custom-call(bf16[4,64,2304]{2,1,0:T(8,128)(2,1)S(1)} %get-tuple-element.10.pay, f32[16,64,128]{2,1,0:T(8,128)S(1)} %broadcast_in_dim.66.allow), custom_call_target="tpu_custom_call" | custom-call | tf_op jit(solution)/shard_map/pallas_call | solution.py:642
  73.7 75.4 %shard_map.104 = (bf16[4,64,2304]{2,1,0:T(8,128)(2,1)S(1)}, f32[72,2304]{1,0:T(8,128)S(1)}) custom-call(bf16[4,64,2304]{2,1,0:T(8,128)(2,1)S(1)} %shard_map.103.res, bf16[4,2,288,256]{3,2,1,0:T(8,128)(2,1)S(1)} %bitcast.56), custom_call_target="tpu_custom_call" | custom-call | flops 1358954496 | bytes 2359296 | tf_op jit(solution)/shard_map/pallas_call | solution.py:550
  149.1 0.3 fusion.28
  149.4 0.7 fusion.17
  150.2 0.7 convolution_add_fusion.1
  150.9 0.7 fusion.1
  151.7 0.3 copy-done.4
  152.0 0.4 fusion.7
  152.3 1.3 fusion.13
  153.6 1.5 fusion.2
  155.1 1.0 slice.34
  156.1 0.7 slice.35
  (45 shorter events, 1.2 us)
Async XLA Ops:
  1.9 1.6 %copy-start.5 = (bf16[1,256,1152]{2,1,0:T(8,128)(2,1)S(1)}, bf16[1,256,1152]{2,1,0:T(8,128)(2,1)}, u32[]{:S(2)}) copy-start(bf16[1,256,1152]{2,1,0:T(8,128)(2,1)} %param.13) | copy-start | bytes 1769476
  3.9 1.0 copy-start.6
  3.9 1.0 copy-start.7
  4.9 0.7 copy-start.10
  5.0 62.8 %copy-start.9 = (s32[1,2,2]{2,1,0:T(2,128)S(1)}, s32[1,2,2]{2,1,0:T(2,128)}, u32[]{:S(2)}) copy-start(s32[1,2,2]{2,1,0:T(2,128)} %param.11) | copy-start | bytes 52
  64.2 2.3 %copy-start = (bf16[3,16,72,768]{3,2,1,0:T(8,128)(2,1)}, bf16[3,16,72,768]{3,2,1,0:T(8,128)(2,1)S(1)}, u32[]{:S(2)}) copy-start(bf16[3,16,72,768]{3,2,1,0:T(8,128)(2,1)S(1)} %get-tuple-element.14) | copy-start | bytes 15925252
  66.5 1.1 copy-start.2
  68.2 5.4 %copy-start.3 = (bf16[4,2,4,72,256]{4,3,2,1,0:T(8,128)(2,1)S(1)}, bf16[4,2,4,72,256]{4,3,2,1,0:T(8,128)(2,1)}, u32[]{:S(2)}) copy-start(bf16[4,2,4,72,256]{4,3,2,1,0:T(8,128)(2,1)} %copy-done.2) | copy-start | bytes 3538948
  68.4 80.6 %copy-start.1 = (bf16[3,16,72,768]{3,2,1,0:T(8,128)(2,1)S(1)}, bf16[3,16,72,768]{3,2,1,0:T(8,128)(2,1)}, u32[]{:S(2)}) copy-start(bf16[3,16,72,768]{3,2,1,0:T(8,128)(2,1)} %copy-done) | copy-start | bytes 15925252
  150.9 1.1 copy-start.4
  150.9 1.1 copy-start.8
